TPU v7x, 128 devices: a whole 4x4x4 slice. The times are simulated.
128 devices in a mesh: dp: 16 (over y, x), expert: 8 (over z, core).
Axes of the slice: x: 4, y: 4, z: 4, core: 2. Of those that a mesh axis runs over, the one named last changes fastest.
Arguments:
- tokens: bfloat16 [16384, 1280], P(('dp', 'expert')), may hold values from -6 to 6
- cotangent: bfloat16 [16384, 1280], P(('dp', 'expert')), may hold values from -4 to 4
- gate_weights: float32 [16384, 2], P(('dp', 'expert')), may hold values from 0.1 to 1
- expert_ids: int32 [16384, 2], P(('dp', 'expert')), may hold values from 0 to 15, as said below
- segments: int32 [128, 128], P(('dp', 'expert')), may hold values from 0 to 3, never falling along the last dimension, each value on 1 to 64 neighbouring positions
- keep_counts: int32 [128, 4], P(('dp', 'expert')), may hold values from 1 to 64
- expand_weight: bfloat16 [16, 2560, 1280], P('expert', 'dp'), may hold values from -0.15625 to 0.15625
- reduce_weight: bfloat16 [16, 2560, 1280], P('expert', 'dp'), may hold values from -0.125 to 0.125
Outputs:
- output: bfloat16 [16384, 1280], P(('dp', 'expert'))
- tokens_grad: bfloat16 [16384, 1280], P(('dp', 'expert'))
- gating_grad: float32 [16384, 2], P(('dp', 'expert'))
- expand_grad: bfloat16 [16, 2560, 1280], P('expert', 'dp')
- reduce_grad: bfloat16 [16, 2560, 1280], P('expert', 'dp')
Inputs may be any that keep to these rules, and one draw needn't show every extreme that they name: `expert_ids`: the 128 tokens of one sequence name each expert exactly 16 times, and a token's 2 experts differ. `segments`: within a sequence the ids never fall, every image 0 to 3 appears, each holds 1 to 64 positions.
All inputs are finite; a program needn't handle non-finite values.
Results may differ from a plain program's by a relative error of at most 0.015.
Values may be sent and summed in bfloat16 or wider, within the bound.
A program may use at most 128 MiB of HBM per device.

v0:
```python
import jax
import jax.numpy as jnp
from jax import lax
from jax.sharding import PartitionSpec as P

epsilon = 1e-06
root_half = 0.7071067811865476
density_scale = 0.3989422804014327


def gelu_value(values):
    return 0.5 * values * (1.0 + jax.scipy.special.erf(values * root_half))


def gelu_slope(values):
    return (
        0.5 * (1.0 + jax.scipy.special.erf(values * root_half))
        + values * jnp.exp(-0.5 * values * values) * density_scale
    )


def project_up(rows, weight):
    return jnp.einsum("rld,lhd->rlh", rows, weight, preferred_element_type=jnp.float32)


def project_down(hidden, weight):
    return jnp.einsum("rlh,lhd->rld", hidden, weight, preferred_element_type=jnp.float32)


def outer_rows(left, right):
    return jnp.einsum("rlh,rld->lhd", left, right, preferred_element_type=jnp.float32)


def body(
    tokens, cotangent, gate_weights, expert_ids, segments, keep_counts, expand_weight, reduce_weight
):
    tok_count = tokens.shape[0]
    top_count = expert_ids.shape[1]
    width = tokens.shape[1]
    sources = lax.axis_size("expert")
    local = expand_weight.shape[0]
    total_experts = local * sources
    pick_count = top_count * tok_count
    capacity = pick_count // total_experts
    image_ids = segments[0]
    position = jnp.arange(tok_count, dtype=jnp.int32)
    earlier_img = jnp.sum((image_ids[None, :] < image_ids[:, None]).astype(jnp.int32), axis=1)
    image_match = (
        image_ids[:, None] == jnp.arange(keep_counts.shape[1], dtype=jnp.int32)[None, :]
    ).astype(jnp.int32)
    keep_token = jnp.sum(image_match * keep_counts, axis=1)
    alive = (position - earlier_img < keep_token).astype(jnp.float32)
    tokens_wide = tokens.astype(jnp.float32)
    mean_rows = jnp.mean(tokens_wide, axis=1, keepdims=True)
    centred = tokens_wide - mean_rows
    inv_scale = lax.rsqrt(jnp.mean(centred * centred, axis=1, keepdims=True) + epsilon)
    normed = centred * inv_scale
    normed_low = normed.astype(jnp.bfloat16)
    choice_list = expert_ids.reshape(-1)
    matches = (choice_list[:, None] == jnp.arange(total_experts, dtype=jnp.int32)[None, :]).astype(
        jnp.int32
    )
    before = jnp.cumsum(matches, axis=0) - matches
    slot_list = jnp.sum(before * matches, axis=1)
    target = choice_list * capacity + slot_list
    order = (
        jnp.zeros((pick_count,), jnp.int32).at[target].set(jnp.arange(pick_count, dtype=jnp.int32))
    )
    source = order // top_count
    alive_pick = jnp.repeat(alive, top_count)
    weight_pick = gate_weights.reshape(-1) * alive_pick
    sent_rows = jnp.where(
        alive_pick[order][:, None] > 0, normed_low[source], jnp.zeros((), jnp.bfloat16)
    )
    cot_wide = cotangent.astype(jnp.float32)
    sent_grads = (cot_wide[source] * weight_pick[order][:, None]).astype(jnp.bfloat16)

    def to_slots(flat):
        return (
            flat.reshape(sources, local, capacity, width)
            .transpose(0, 2, 1, 3)
            .reshape(sources * capacity, local, width)
        )

    def from_slots(rows):
        return (
            rows.reshape(sources, capacity, local, width)
            .transpose(0, 2, 1, 3)
            .reshape(pick_count, width)
        )

    arrived = to_slots(lax.all_to_all(sent_rows, "expert", split_axis=0, concat_axis=0, tiled=True))
    arrived_grads = to_slots(
        lax.all_to_all(sent_grads, "expert", split_axis=0, concat_axis=0, tiled=True)
    )
    slot_rows = arrived.shape[0]
    all_rows = lax.all_gather(arrived, "dp", axis=0, tiled=True)
    pre = project_up(all_rows, expand_weight)
    hidden = gelu_value(pre).astype(jnp.bfloat16)
    results = lax.psum_scatter(
        project_down(hidden, reduce_weight).astype(jnp.bfloat16),
        "dp",
        scatter_dimension=0,
        tiled=True,
    )
    all_grads = lax.all_gather(arrived_grads, "dp", axis=0, tiled=True)
    back_hidden = project_up(all_grads, reduce_weight)
    dpre = (back_hidden * gelu_slope(pre)).astype(jnp.bfloat16)
    input_rows = lax.psum_scatter(
        project_down(dpre, expand_weight).astype(jnp.bfloat16),
        "dp",
        scatter_dimension=0,
        tiled=True,
    )

    def add_block(block, totals):
        offset = block * slot_rows
        hidden_block = lax.dynamic_slice_in_dim(hidden, offset, slot_rows, 0)
        dpre_block = lax.dynamic_slice_in_dim(dpre, offset, slot_rows, 0)
        grad_block = lax.dynamic_slice_in_dim(all_grads, offset, slot_rows, 0)
        row_block = lax.dynamic_slice_in_dim(all_rows, offset, slot_rows, 0)
        second_piece = lax.optimization_barrier(
            outer_rows(hidden_block, grad_block).astype(jnp.bfloat16)
        ).astype(jnp.float32)
        first_piece = lax.optimization_barrier(
            outer_rows(dpre_block, row_block).astype(jnp.bfloat16)
        ).astype(jnp.float32)
        return (totals[0] + first_piece, totals[1] + second_piece)

    empty = jnp.zeros(expand_weight.shape, jnp.float32)
    first_total, second_total = lax.fori_loop(
        0, all_rows.shape[0] // slot_rows, add_block, (empty, empty)
    )
    expand_grad = first_total.astype(jnp.bfloat16)
    reduce_grad = second_total.astype(jnp.bfloat16)
    returned = lax.all_to_all(
        from_slots(results), "expert", split_axis=0, concat_axis=0, tiled=True
    )
    result_pick = returned[target].astype(jnp.float32).reshape(tok_count, top_count, -1)
    output = (
        tokens_wide + jnp.sum(result_pick * weight_pick.reshape(tok_count, top_count, 1), axis=1)
    ).astype(jnp.bfloat16)
    gating_grad = alive_pick.reshape(tok_count, top_count) * jnp.sum(
        cot_wide[:, None, :] * result_pick, axis=2
    )
    returned_grads = lax.all_to_all(
        from_slots(input_rows), "expert", split_axis=0, concat_axis=0, tiled=True
    )
    input_pick = returned_grads[target].astype(jnp.float32).reshape(tok_count, top_count, -1)
    grad_norm = jnp.sum(input_pick * alive_pick.reshape(tok_count, top_count, 1), axis=1)
    tokens_grad = cot_wide + inv_scale * (
        grad_norm
        - jnp.mean(grad_norm, axis=1, keepdims=True)
        - normed * jnp.mean(grad_norm * normed, axis=1, keepdims=True)
    )
    return (output, tokens_grad.astype(jnp.bfloat16), gating_grad, expand_grad, reduce_grad)


def solution(mesh):
    in_specs = (
        P(("dp", "expert"), None),
        P(("dp", "expert"), None),
        P(("dp", "expert"), None),
        P(("dp", "expert"), None),
        P(("dp", "expert"), None),
        P(("dp", "expert"), None),
        P("expert", "dp", None),
        P("expert", "dp", None),
    )
    out_specs = (
        P(("dp", "expert"), None),
        P(("dp", "expert"), None),
        P(("dp", "expert"), None),
        P("expert", "dp", None),
        P("expert", "dp", None),
    )
    return jax.shard_map(body, mesh=mesh, in_specs=in_specs, out_specs=out_specs, check_vma=False)
```

profile of v0, /device:TPU:1, one launch (start us, length us, event | category | flops | bytes accessed | tf_op | source)
XLA Modules:
  0.0 435.0 jit_solution(15564184737724795476)
XLA Ops:
  16.0 1.9 gather_fusion
  19.6 17.6 %all_to_all.36 = bf16[8,32,1280]{2,1,0:T(8,128)(2,1)S(1)} all-to-all(bf16[8,32,1280]{2,1,0:T(8,128)(2,1)S(1)} %broadcast_select_fusion), channel_id=1, replica_groups=mesh['dp'=16,'expert'=8] {'expert'}, dimensions={0} | all-to-all | bytes 1310720 | tf_op jit(solution)/shard_map/all_to_all | solution.py:92
  38.4 1.9 gather_fusion.4
  41.9 14.2 %all_to_all.37 = bf16[8,32,1280]{2,1,0:T(8,128)(2,1)S(1)} all-to-all(bf16[8,32,1280]{2,1,0:T(8,128)(2,1)S(1)} %multiply_convert_fusion.1), channel_id=1, replica_groups=mesh['dp'=16,'expert'=8] {'expert'}, dimensions={0} | all-to-all | bytes 1310720 | tf_op jit(solution)/shard_map/all_to_all | solution.py:94
  57.1 61.1 %all-gather.3.cloned.1.call-done = bf16[2048,2,1280]{2,0,1:T(8,128)(2,1)} async-done(((bf16[128,2,1280]{2,0,1:T(8,128)(2,1)}), bf16[2048,2,1280]{2,0,1:T(8,128)(2,1)}) %all-gather.3.cloned.1.call-update) | async-done | bytes 10485776 | tf_op jit(solution)/shard_map/all_gather | solution.py:97
  118.2 9.1 %multiply_convert_fusion = (bf16[2048,2,160]{0,2,1:T(8,128)(2,1)S(1)}, f32[2048,2,160]{0,2,1:T(8,128)}) fusion(bf16[2048,2,1280]{2,0,1:T(8,128)(2,1)} %all-gather.3.cloned.1.call-done, bf16[2,160,1280]{2,1,0:T(8,128)(2,1)S(1)} %copy-done), kind=kOutput, calls=%fused_computation.30 | convolution fusion | flops 1680998400 | bytes 15237120 | tf_op jit(solution)/shard_map/rld,lhd->rlh/dot_general | solution.py:23
  127.3 73.6 %all-gather.5.cloned.1.call-done = bf16[2048,2,1280]{2,0,1:T(8,128)(2,1)} async-done(((bf16[128,2,1280]{2,0,1:T(8,128)(2,1)}), bf16[2048,2,1280]{2,0,1:T(8,128)(2,1)}) %all-gather.5.cloned.1.call-update) | async-done | bytes 10485776 | tf_op jit(solution)/shard_map/all_gather | solution.py:106
  200.9 8.6 %fusion.9 = bf16[2048,2,160]{0,2,1:T(8,128)(2,1)S(1)} fusion(bf16[2048,2,1280]{2,0,1:T(8,128)(2,1)} %all-gather.5.cloned.1.call-done, bf16[2,160,1280]{2,1,0:T(8,128)(2,1)} %param.17, f32[2048,2,160]{0,2,1:T(8,128)} %get-tuple-element.189), kind=kOutput, calls=%fused_computation.25 | convolution fusion | flops 1684275200 | bytes 15237120 | tf_op jit(solution)/shard_map/rld,lhd->rlh/dot_general | solution.py:23
  210.6 5.6 %fusion.7 = bf16[2048,2,1280]{2,0,1:T(8,128)(2,1)} fusion(bf16[2048,2,160]{0,2,1:T(8,128)(2,1)S(1)} %fusion.9, bf16[2,160,1280]{2,1,0:T(8,128)(2,1)S(1)} %copy-done), kind=kOutput, calls=%fused_computation.20 | convolution fusion | flops 1682964480 | bytes 12615680 | tf_op jit(solution)/shard_map/rlh,lhd->rld/dot_general | solution.py:27
  217.3 5.7 %fusion.6 = bf16[2048,2,1280]{2,0,1:T(8,128)(2,1)} fusion(bf16[2048,2,160]{0,2,1:T(8,128)(2,1)S(1)} %get-tuple-element.244, bf16[2,160,1280]{2,1,0:T(8,128)(2,1)S(1)} %copy-done.10), kind=kOutput, calls=%fused_computation.19 | convolution fusion | flops 1682964480 | bytes 12615680 | tf_op jit(solution)/shard_map/rlh,lhd->rld/dot_general | solution.py:27
  223.1 81.9 %reduce-scatter.5.cloned.1.call-done = bf16[128,2,1280]{2,0,1:T(8,128)(2,1)} async-done(((bf16[2048,2,1280]{2,0,1:T(8,128)(2,1)}), bf16[128,2,1280]{2,0,1:T(8,128)(2,1)}) %reduce-scatter.5.cloned.1.call-update) | async-done | bytes 655376 | tf_op jit(solution)/shard_map/reduce_scatter | solution.py:109
  305.0 2.0 copy.47
  307.0 6.0 %all-to-all-start.3 = ((bf16[8,32,1280]{2,1,0:T(8,128)(2,1)}), bf16[8,32,1280]{2,1,0:T(8,128)(2,1)}, u32[]{:S(2)}, u32[]{:S(2)}) async-start(bf16[8,32,1280]{2,1,0:T(8,128)(2,1)} %bitcast.23), calls=%async_computation.5 | async-start | bytes 1310720 | tf_op jit(solution)/shard_map/all_to_all | solution.py:146
  313.0 86.8 %while.16 = (s32[]{:T(128)}, f32[2,160,1280]{2,1,0:T(8,128)}, f32[2,160,1280]{2,1,0:T(8,128)S(1)}, bf16[2048,2,160]{0,2,1:T(8,128)(2,1)}, bf16[2048,2,1280]{2,0,...) while((s32[]{:T(128)}, f32[2,160,1280]{2,1,0:T(8,128)}, ...), condition=%wide.region_17.18_spmd.clone, body=%wide.region_16.17_spmd.clone.sunk | while | flops 212992000 | bytes 24414436 | solution.py:131
  361.9 1.6 convolution_convert_fusion.6
  367.3 1.6 convolution_convert_fusion.6
  402.5 2.0 copy.42
  404.5 4.7 %all-to-all-start.1 = ((bf16[8,32,1280]{2,1,0:T(8,128)(2,1)}), bf16[8,32,1280]{2,1,0:T(8,128)(2,1)S(1)}, u32[]{:S(2)}, u32[]{:S(2)}) async-start(bf16[8,32,1280]{2,1,0:T(8,128)(2,1)} %bitcast.13), calls=%async_computation.2 | async-start | bytes 1310720 | tf_op jit(solution)/shard_map/all_to_all | solution.py:136
  409.2 2.9 gather_fusion.5
  412.5 1.7 reshape.174
  414.3 3.0 multiply_reduce_fusion.2
  417.7 2.5 all-to-all-done.1
  421.4 1.7 reshape.173
  423.1 3.5 multiply_reduce_fusion
  (197 shorter events, 105.9 us)
Async XLA Ops:
  7.2 111.0 %copy-start = (bf16[2,160,1280]{2,1,0:T(8,128)(2,1)S(1)}, bf16[2,160,1280]{2,1,0:T(8,128)(2,1)}, u32[]{:S(2)}) copy-start(bf16[2,160,1280]{2,1,0:T(8,128)(2,1)} %param.16) | copy-start | bytes 2457604
  7.2 10.8 %copy-start.5 = (bf16[128,1280]{1,0:T(8,128)(2,1)S(1)}, bf16[128,1280]{1,0:T(8,128)(2,1)}, u32[]{:S(2)}) copy-start(bf16[128,1280]{1,0:T(8,128)(2,1)} %param.10) | copy-start | bytes 983044
  7.2 111.0 %all-gather.3.cloned.1.call-start = ((), (), s32[]{:S(2)}) async-start(), calls=%async_computation.6 | async-start | bytes 11141120 | tf_op jit(solution)/shard_map/all_gather | solution.py:97
  19.6 18.5 %copy-start.11 = (f32[128,2]{0,1:T(2,128)S(1)}, f32[128,2]{0,1:T(2,128)}, u32[]{:S(2)}) copy-start(f32[128,2]{0,1:T(2,128)} %param.12) | copy-start | bytes 3076
  37.2 3.3 copy-start.8
  38.1 162.8 %all-gather.5.cloned.1.call-start = ((), (), s32[]{:S(2)}) async-start(), calls=%async_computation.8 | async-start | bytes 11141120 | tf_op jit(solution)/shard_map/all_gather | solution.py:106
  57.0 248.0 %reduce-scatter.5.cloned.1.call-start = ((), (), s32[]{:S(2)}) async-start(), calls=%async_computation.9 | async-start | bytes 11141120 | tf_op jit(solution)/shard_map/reduce_scatter | solution.py:109
  127.3 89.1 %copy-start.6 = (bf16[2048,2,160]{0,2,1:T(8,128)(2,1)}, bf16[2048,2,160]{0,2,1:T(8,128)(2,1)S(1)}, u32[]{:S(2)}) copy-start(bf16[2048,2,160]{0,2,1:T(8,128)(2,1)S(1)} %get-tuple-element.244) | copy-start | bytes 3932164
  216.2 186.3 %reduce-scatter.3.cloned.1.call-start = ((), (), s32[]{:S(2)}) async-start(), calls=%async_computation.7 | async-start | bytes 11141120 | tf_op jit(solution)/shard_map/reduce_scatter | solution.py:100
  307.0 97.5 %all-to-all-start.3 = ((bf16[8,32,1280]{2,1,0:T(8,128)(2,1)}), bf16[8,32,1280]{2,1,0:T(8,128)(2,1)}, u32[]{:S(2)}, u32[]{:S(2)}) async-start(bf16[8,32,1280]{2,1,0:T(8,128)(2,1)} %bitcast.23), calls=%async_computation.5 | async-start | bytes 1310720 | tf_op jit(solution)/shard_map/all_to_all | solution.py:146
  318.4 3.1 copy-start.2
  323.8 3.2 copy-start.2
  329.2 3.2 copy-start.2
  334.8 3.1 copy-start.2
  340.2 3.2 copy-start.2
  345.6 3.1 copy-start.2
  351.1 3.1 copy-start.2
  361.9 3.2 copy-start.2
  367.3 3.1 copy-start.2
  388.9 3.2 copy-start.2
  394.4 3.2 copy-start.2
  404.5 15.6 %all-to-all-start.1 = ((bf16[8,32,1280]{2,1,0:T(8,128)(2,1)}), bf16[8,32,1280]{2,1,0:T(8,128)(2,1)S(1)}, u32[]{:S(2)}, u32[]{:S(2)}) async-start(bf16[8,32,1280]{2,1,0:T(8,128)(2,1)} %bitcast.13), calls=%async_computation.2 | async-start | bytes 1310720 | tf_op jit(solution)/shard_map/all_to_all | solution.py:136
  423.1 4.2 copy-start.9
  423.1 5.4 %copy-start.1 = (bf16[2,160,1280]{2,1,0:T(8,128)(2,1)S(1)}, bf16[2,160,1280]{2,1,0:T(8,128)(2,1)}, u32[]{:S(2)}) copy-start(bf16[2,160,1280]{2,1,0:T(8,128)(2,1)} %param.16) | copy-start | bytes 2457604
  (24 other events, 38.6 us)
Sparse Core Ops, SparseCore 0:
  38.2 79.9 all-gather.2
  120.9 79.9 all-gather.4
  216.3 88.6 reduce-scatter.4
  308.3 89.1 reduce-scatter.2
where the time goes:
time: 437 us; the launch traced here: 435 us
  waiting for transfers between devices  219 us (50%)
  matrix products  79 us (18%)
  local copies, waits for them, and re-layouts  45.8 us (10%)
  other arithmetic  33.5 us (8%)
  blocking collectives  31.8 us (7%)
  between operations  14 us (3%)
  starting transfers between devices  11.1 us (3%)
    reduce_scatter x1, waiting for transfers between devices, body(): lax.psum_scatter(project_down(dpre, expand_weight).astype(jnp.bfloat16),...  81.9 us
    all_gather x1, waiting for transfers between devices, body(): all_grads = lax.all_gather(arrived_grads, 'dp', axis=0, tiled=True)  73.6 us
    all_gather x1, waiting for transfers between devices, body(): all_rows = lax.all_gather(arrived, 'dp', axis=0, tiled=True)  61.1 us
    dot_general x32, matrix products, outer_rows(): jnp.einsum('rlh,rld->lhd', left, right, preferred_element_type=jnp.float32)  50.1 us
    while x64, local copies, waits for them, and re-layouts  19 us
    dot_general x2, matrix products, project_up(): jnp.einsum('rld,lhd->rlh', rows, weight, preferred_element_type=jnp.float32)  17.7 us
    all_to_all x1, blocking collectives, body(): lax.all_to_all(sent_rows, 'expert', split_axis=0, concat_axis=0, tiled=True)  17.6 us
    add x16, other arithmetic, add_block(): return (totals[0] + first_piece, totals[1] + second_piece)  17.2 us
  transfers between devices with their start and end apart: 6, of which 4 were waited for; matrix products, arithmetic and copies ran while one was open for 23% of the time, Pallas kernels for 0%

commit v1 on v0

v1 whole, which is shorter than its diff:
```python
import jax
import jax.numpy as jnp
from jax import lax
from jax.experimental import pallas as pl
from jax.experimental.pallas import tpu as pltpu
from jax.sharding import PartitionSpec as P

MESH = pl.DeviceIdType.MESH
epsilon = 1e-06
root_half = 0.7071067811865476
density_scale = 0.3989422804014327

D = 1280
TOK = 128
SLOTS = 256
CAP = 16
NE = 16
SH = 160
HS = SH // 2
Q = 4 * HS
HID = 4 * Q
ROWS = 2 * SLOTS
BF = jnp.bfloat16
F32 = jnp.float32


def dot(a, b, ca, cb):
    return lax.dot_general(a, b, (((ca,), (cb,)), ((), ())), preferred_element_type=F32)


def kernel(
    tok, cot, gw, ids, seg, keep, w1_in, w2_in,
    out, tg, gg, eg, rg,
    pt, normed, inv, wcol, acol, xs, gs, x_all, g_all, w1, w2, hid, slope, dpre, trans,
    y_send, y_own, y_recv, y_fin, y_ret, d_send, d_own, d_recv, d_fin, d_ret,
    e_own, e_send, e_core, e_wp, e_far, e_fin, r_own, r_send, r_core, r_wp, r_far, r_fin,
    a_ss, a_rs, b_ss, b_rs, w_ss, w_rs, wy_ss, wy_rs, wc_ss, wc_rs,
    gc_ss, gc_rs, gy_ss, gy_rs, gx_ss, gx_rs,
):
    dp = lax.axis_index("dp")
    ex = lax.axis_index("expert")
    y, x = dp // 4, dp % 4
    z, c = ex // 2, ex % 2
    me = z * 4 + x
    row_mate = y + 1 - 2 * (y % 2)
    wgt_mate = (y + 5 - 2 * ((y + 1) % 2)) % 4
    other = 1 - c

    def dev(yy, xx, zz, cc):
        return (yy * 4 + xx, zz * 2 + cc)

    row_dev = dev(row_mate, x, z, c)
    wgt_dev = dev(wgt_mate, x, z, c)
    core_dev = dev(y, x, z, other)

    def remote(src, dst, ss, rs, target):
        return pltpu.make_async_remote_copy(
            src_ref=src, dst_ref=dst, send_sem=ss, recv_sem=rs, device_id=target, device_id_type=MESH
        )

    def arrived(dst, rs):
        pltpu.make_async_copy(dst, dst, rs).wait()

    def blk(ref, i, n):
        return ref.at[pl.ds(pl.multiple_of(i * n, n), n)]

    barrier = pltpu.get_barrier_semaphore()
    for i in range(1, NE):
        t = (me + i) % NE
        pl.semaphore_signal(barrier, inc=1, device_id=dev(y, t % 4, t // 4, c), device_id_type=MESH)
    for i in range(4):
        pl.semaphore_signal(barrier, inc=1, device_id=dev(y, i, z, other), device_id_type=MESH)
    for target in (row_dev, wgt_dev):
        pl.semaphore_signal(barrier, inc=1, device_id=target, device_id_type=MESH)
    pl.semaphore_wait(barrier, NE - 1 + 4 + 2)

    def weights_x(m, w_in, w, act):
        for l in range(2):
            for h in range(2):
                tx = 2 * c + l
                src = w_in.at[l, pl.ds(HS * h, HS)]
                dst = blk(w, x, HS)
                own = jnp.logical_and(tx == x, h == c)

                @pl.when(own)
                def _():
                    if act == "start":
                        pltpu.make_async_copy(src, dst, w_rs.at[m, x]).start()

                @pl.when(jnp.logical_not(own))
                def _():
                    copy = remote(src, dst, w_ss.at[m, 2 * l + h], w_rs.at[m, x], dev(y, tx, z, h))
                    copy.start() if act == "start" else copy.wait_send()

    weights_x(0, w1_in, w1, "start")
    weights_x(1, w2_in, w2, "start")

    def swap_blocks(k, src, dst, act):
        if act == "start":
            pltpu.make_async_copy(blk(src, me, CAP), blk(dst, me, CAP), a_rs.at[k, 0]).start()
        for i in range(1, NE):
            t = (me + i) % NE
            copy = remote(
                blk(src, t, CAP), blk(dst, me, CAP), a_ss.at[k, i], a_rs.at[k, i], dev(y, t % 4, t // 4, c)
            )
            copy.start() if act == "start" else copy.wait_send()

    def swap_wait(k, dst):
        for i in range(NE):
            arrived(blk(dst, (me + NE - i) % NE, CAP), a_rs.at[k, i])

    lane = lax.broadcasted_iota(jnp.int32, (TOK, TOK), 1)
    sub = lax.broadcasted_iota(jnp.int32, (TOK, TOK), 0)
    seg_row = jnp.broadcast_to(seg[...].astype(F32), (TOK, TOK))
    seg_col = jnp.sum(jnp.where(lane == sub, seg_row, 0.0), axis=1, keepdims=True)
    earlier = jnp.sum((seg_row < seg_col).astype(F32), axis=1, keepdims=True)
    images = keep.shape[1]
    image = lax.broadcasted_iota(jnp.int32, (TOK, images), 1).astype(F32)
    kept = jnp.broadcast_to(keep[...].astype(F32), (TOK, images))
    keep_token = jnp.sum(jnp.where(image == seg_col, kept, 0.0), axis=1, keepdims=True)
    position = lax.broadcasted_iota(jnp.int32, (TOK, 1), 0).astype(F32)
    alive = (position - earlier < keep_token).astype(F32)
    acol[...] = alive
    wcol[...] = gw[...] * alive
    expert = lax.broadcasted_iota(jnp.int32, (TOK, NE), 1)
    match = [(ids[:, k : k + 1] == expert).astype(F32) for k in range(2)]
    before = dot((lane < sub).astype(BF), (match[0] + match[1]).astype(BF), 1, 0)
    slot_iota = lax.broadcasted_iota(jnp.int32, (TOK, SLOTS), 1).astype(F32)
    for k in range(2):
        slot = jnp.sum(before * match[k], axis=1, keepdims=True)
        if k == 1:
            slot = slot + jnp.sum(match[0] * match[1], axis=1, keepdims=True)
        target_slot = ids[:, k : k + 1].astype(F32) * CAP + slot
        pt[k] = (slot_iota == target_slot).astype(BF)

    wide = tok[...].astype(F32)
    centred = wide - jnp.mean(wide, axis=1, keepdims=True)
    scale = lax.rsqrt(jnp.mean(centred * centred, axis=1, keepdims=True) + epsilon)
    inv[...] = scale
    normed[...] = centred * scale
    feats = (normed[...].astype(BF).astype(F32) * alive).astype(BF)
    xs[...] = dot(pt[0] + pt[1], feats, 0, 0).astype(BF)
    swap_blocks(0, xs, x_all, "start")
    grads = [(cot[...].astype(F32) * wcol[:, k : k + 1]).astype(BF) for k in range(2)]
    gs[...] = (dot(pt[0], grads[0], 0, 0) + dot(pt[1], grads[1], 0, 0)).astype(BF)
    swap_blocks(1, gs, g_all, "start")

    own_rows, mate_rows = pl.ds(0, SLOTS), pl.ds(SLOTS, SLOTS)

    def rows_y(k, src, dst):
        return remote(src, dst, b_ss.at[k], b_rs.at[k], row_dev)

    def quarter(w, s, h):
        return w.at[pl.ds((2 * s + h) * Q, Q)]

    def weights_y(m, w):
        return remote(quarter(w, 0, 0), quarter(w, 1, 0), wy_ss.at[m], wy_rs.at[m], wgt_dev)

    def weights_core(m, w, s):
        return remote(quarter(w, s, 0), quarter(w, s, 1), wc_ss.at[m, s], wc_rs.at[m, s], core_dev)

    def weights_mid(m, w):
        for i in range(4):
            arrived(w.at[pl.ds(i * HS, HS)], w_rs.at[m, i])
        weights_y(m, w).start()
        weights_core(m, w, 0).start()

    def weights_last(m, w):
        weights_y(m, w).wait_recv()
        weights_core(m, w, 1).start()

    swap_wait(0, x_all)
    rows_y(0, x_all.at[own_rows], x_all.at[mate_rows]).start()
    weights_mid(0, w1)
    swap_wait(1, g_all)
    rows_y(1, g_all.at[own_rows], g_all.at[mate_rows]).start()
    weights_mid(1, w2)
    weights_last(0, w1)
    rows_y(0, x_all.at[own_rows], x_all.at[mate_rows]).wait_recv()
    weights_core(0, w1, 0).wait_recv()
    weights_core(0, w1, 1).wait_recv()

    def tile(j, n=256):
        return pl.ds(pl.multiple_of(j * n, n), n)

    @pl.loop(0, HID // 256)
    def _(j):
        pre = dot(x_all[...], w1[tile(j), :], 1, 1)
        cdf = 0.5 * (1.0 + lax.erf(pre * root_half))
        hid[:, tile(j)] = (pre * cdf).astype(BF)
        slope[:, tile(j)] = cdf + pre * jnp.exp(-0.5 * pre * pre) * density_scale

    weights_last(1, w2)
    weights_core(1, w2, 0).wait_recv()
    weights_core(1, w2, 1).wait_recv()

    @pl.loop(0, D // 256)
    def _(n):
        y_send[:, tile(n)] = dot(hid[mate_rows, :], w2[:, tile(n)], 1, 0).astype(BF)

    rows_y(2, y_send, y_recv).start()

    @pl.loop(0, D // 256)
    def _(n):
        y_own[:, tile(n)] = dot(hid[own_rows, :], w2[:, tile(n)], 1, 0)

    rows_y(1, g_all.at[own_rows], g_all.at[mate_rows]).wait_recv()

    @pl.loop(0, HID // 256)
    def _(j):
        back = dot(g_all[...], w2[tile(j), :], 1, 1)
        dpre[:, tile(j)] = (back * slope[:, tile(j)]).astype(BF)

    @pl.loop(0, D // 256)
    def _(n):
        d_send[:, tile(n)] = dot(dpre[mate_rows, :], w1[:, tile(n)], 1, 0).astype(BF)

    rows_y(3, d_send, d_recv).start()

    @pl.loop(0, D // 256)
    def _(n):
        d_own[:, tile(n)] = dot(dpre[own_rows, :], w1[:, tile(n)], 1, 0)

    def rows_back(k, own, send, recv, fin, ret):
        rows_y(k, send, recv).wait_recv()

        @pl.loop(0, SLOTS // 64)
        def _(i):
            fin[tile(i, 64), :] = (own[tile(i, 64), :] + recv[tile(i, 64), :].astype(F32)).astype(BF)

        swap_blocks(k, fin, ret, "start")

    rows_back(2, y_own, y_send, y_recv, y_fin, y_ret)

    def grads_core(m, send, core, s):
        return remote(send.at[s], core.at[s], gc_ss.at[m, s], gc_rs.at[m, s], core_dev)

    def weight_grads(m, left, right, own, send, core):
        @pl.loop(0, HID // 256)
        def _(j):
            trans[tile(j), :] = left[:, tile(j)].T

        for s in (1, 0):

            @pl.loop(0, D // 256)
            def _(n):
                part = dot(trans[pl.ds(s * 2 * Q, 2 * Q), :], right[:, tile(n)], 1, 0)
                own[s, :, tile(n)] = part[:Q]
                send[s, :, tile(n)] = part[Q:].astype(BF)

            grads_core(m, send, core, s).start()

    def grads_y(m, wp, far):
        return remote(wp, far, gy_ss.at[m], gy_rs.at[m], wgt_dev)

    def grads_mid(m, own, send, core, wp, far):
        grads_core(m, send, core, 1).wait_recv()

        @pl.loop(0, Q // 80)
        def _(i):
            wp[tile(i, 80), :] = (own[1, tile(i, 80), :] + core[1, tile(i, 80), :].astype(F32)).astype(BF)

        grads_y(m, wp, far).start()

    def grads_x(m, fin, result, act):
        for i in range(4):
            src = fin.at[pl.ds(i * HS, HS)]
            dst = result.at[x % 2, blk_rows(c)]
            own = jnp.logical_and(i == x, c == x // 2)

            @pl.when(own)
            def _():
                if act == "start":
                    pltpu.make_async_copy(src, dst, gx_rs.at[m, 2 * (x % 2) + c]).start()

            @pl.when(jnp.logical_not(own))
            def _():
                copy = remote(
                    src, dst, gx_ss.at[m, i], gx_rs.at[m, 2 * (x % 2) + c], dev(y, i, z, x // 2)
                )
                copy.start() if act == "start" else copy.wait_send()

    def blk_rows(h):
        return pl.ds(pl.multiple_of(h * HS, HS), HS)

    def grads_last(m, own, send, core, wp, far, fin, result):
        grads_core(m, send, core, 0).wait_recv()
        grads_y(m, wp, far).wait_recv()

        @pl.loop(0, Q // 80)
        def _(i):
            r = tile(i, 80)
            fin[r, :] = (own[0, r, :] + core[0, r, :].astype(F32) + far[r, :].astype(F32)).astype(BF)

        grads_x(m, fin, result, "start")

    weight_grads(1, hid, g_all, r_own, r_send, r_core)
    grads_mid(1, r_own, r_send, r_core, r_wp, r_far)
    rows_back(3, d_own, d_send, d_recv, d_fin, d_ret)
    weight_grads(0, dpre, x_all, e_own, e_send, e_core)
    grads_mid(0, e_own, e_send, e_core, e_wp, e_far)
    grads_last(1, r_own, r_send, r_core, r_wp, r_far, r_fin, rg)

    swap_wait(2, y_ret)
    result = tok[...].astype(F32)
    for k in range(2):
        pick = dot(pt[k], y_ret[...], 1, 0)
        result = result + pick * wcol[:, k : k + 1]
        gg[:, k : k + 1] = acol[...] * jnp.sum(cot[...].astype(F32) * pick, axis=1, keepdims=True)
    out[...] = result.astype(BF)
    swap_wait(3, d_ret)
    dnorm = (dot(pt[0], d_ret[...], 1, 0) + dot(pt[1], d_ret[...], 1, 0)) * acol[...]
    tail = dnorm - jnp.mean(dnorm, axis=1, keepdims=True)
    tail = tail - normed[...] * jnp.mean(dnorm * normed[...], axis=1, keepdims=True)
    tg[...] = (cot[...].astype(F32) + inv[...] * tail).astype(BF)

    grads_last(0, e_own, e_send, e_core, e_wp, e_far, e_fin, eg)

    for m, result in ((1, rg), (0, eg)):
        for l in range(2):
            for h in range(2):
                arrived(result.at[l, pl.ds(h * HS, HS)], gx_rs.at[m, 2 * l + h])
    weights_x(0, w1_in, w1, "wait")
    weights_x(1, w2_in, w2, "wait")
    swap_blocks(0, xs, x_all, "wait")
    swap_blocks(1, gs, g_all, "wait")
    swap_blocks(2, y_fin, y_ret, "wait")
    swap_blocks(3, d_fin, d_ret, "wait")
    rows_y(0, x_all.at[own_rows], x_all.at[mate_rows]).wait_send()
    rows_y(1, g_all.at[own_rows], g_all.at[mate_rows]).wait_send()
    rows_y(2, y_send, y_recv).wait_send()
    rows_y(3, d_send, d_recv).wait_send()
    for m, w in ((0, w1), (1, w2)):
        weights_y(m, w).wait_send()
        for s in range(2):
            weights_core(m, w, s).wait_send()
    for m, send, core, wp, far, fin, result in (
        (0, e_send, e_core, e_wp, e_far, e_fin, eg),
        (1, r_send, r_core, r_wp, r_far, r_fin, rg),
    ):
        for s in range(2):
            grads_core(m, send, core, s).wait_send()
        grads_y(m, wp, far).wait_send()
        grads_x(m, fin, result, "wait")


def body(*args):
    vmem = pl.BlockSpec(memory_space=pltpu.VMEM)
    hbm = pl.BlockSpec(memory_space=pl.ANY)
    dma = pltpu.SemaphoreType.DMA
    shape = jax.ShapeDtypeStruct
    grad_scratch = [
        pltpu.VMEM((2, Q, D), F32),
        pltpu.VMEM((2, Q, D), BF),
        pltpu.VMEM((2, Q, D), BF),
        pltpu.VMEM((Q, D), BF),
        pltpu.VMEM((Q, D), BF),
        pltpu.VMEM((Q, D), BF),
    ]
    row_scratch = [
        pltpu.VMEM((SLOTS, D), BF),
        pltpu.VMEM((SLOTS, D), F32),
        pltpu.VMEM((SLOTS, D), BF),
        pltpu.VMEM((SLOTS, D), BF),
        pltpu.VMEM((SLOTS, D), BF),
    ]
    return pl.pallas_call(
        kernel,
        out_shape=(
            shape((TOK, D), BF),
            shape((TOK, D), BF),
            shape((TOK, 2), F32),
            shape((2, SH, D), BF),
            shape((2, SH, D), BF),
        ),
        in_specs=[vmem] * 6 + [hbm] * 2,
        out_specs=(vmem, vmem, vmem, hbm, hbm),
        scratch_shapes=[
            pltpu.VMEM((2, TOK, SLOTS), BF),
            pltpu.VMEM((TOK, D), F32),
            pltpu.VMEM((TOK, 1), F32),
            pltpu.VMEM((TOK, 2), F32),
            pltpu.VMEM((TOK, 1), F32),
            pltpu.VMEM((SLOTS, D), BF),
            pltpu.VMEM((SLOTS, D), BF),
            pltpu.VMEM((ROWS, D), BF),
            pltpu.VMEM((ROWS, D), BF),
            pltpu.VMEM((HID, D), BF),
            pltpu.VMEM((HID, D), BF),
            pltpu.VMEM((ROWS, HID), BF),
            pltpu.VMEM((ROWS, HID), F32),
            pltpu.VMEM((ROWS, HID), BF),
            pltpu.VMEM((HID, ROWS), BF),
        ]
        + row_scratch * 2
        + grad_scratch * 2
        + [
            dma((4, NE)),
            dma((4, NE)),
            dma((4,)),
            dma((4,)),
            dma((2, 4)),
            dma((2, 4)),
            dma((2,)),
            dma((2,)),
            dma((2, 2)),
            dma((2, 2)),
            dma((2, 2)),
            dma((2, 2)),
            dma((2,)),
            dma((2,)),
            dma((2, 4)),
            dma((2, 4)),
        ],
        compiler_params=pltpu.CompilerParams(
            collective_id=0, has_side_effects=True, vmem_limit_bytes=60 * 2**20
        ),
    )(*args)


def solution(mesh):
    rows = P(("dp", "expert"), None)
    weights = P("expert", "dp", None)
    return jax.shard_map(
        body,
        mesh=mesh,
        in_specs=(rows,) * 6 + (weights,) * 2,
        out_specs=(rows,) * 3 + (weights,) * 2,
        check_vma=False,
    )
```

time: 437 us -> 161 us (0.37)
  waiting for transfers between devices: 219 us -> 0 us
  Pallas kernels: 0 us -> 151 us
  matrix products: 79 us -> 0 us
  local copies, waits for them, and re-layouts: 45.8 us -> 9.48 us
  other arithmetic: 33.5 us -> 0 us
  blocking collectives: 31.8 us -> 0 us
  between operations: 14 us -> 0.66 us
  starting transfers between devices: 11.1 us -> 0 us
    pallas_call x0 -> x1, Pallas kernels: none -> 151 us  [body(): pl.pallas_call(kernel, out_shape=(shape((TOK, D), BF), shape((TOK, D), BF...]
    all_gather x2 -> x0, waiting for transfers between devices: 135 us -> none  [the longest x1 73.6 us: body(): all_grads = lax.all_gather(arrived_grads, 'dp', axis=0, tiled=True)]
    reduce_scatter x2 -> x0, waiting for transfers between devices: 81.9 us -> none  [the longest x1 81.9 us: body(): lax.psum_scatter(project_down(dpre, expand_weight).astype(jnp.bfloat16),...]
    dot_general x36 -> x0, matrix products: 79 us -> none  [the longest x32 50.1 us: outer_rows(): jnp.einsum('rlh,rld->lhd', left, right, preferred_element_type=jnp.float32)]
    all_to_all x2 -> x0, blocking collectives: 31.8 us -> none  [the longest x1 17.6 us: body(): lax.all_to_all(sent_rows, 'expert', split_axis=0, concat_axis=0, tiled=True)]
    while x64 -> x0, local copies, waits for them, and re-layouts: 19 us -> none
    add x16 -> x0, other arithmetic: 17.2 us -> none  [add_block(): return (totals[0] + first_piece, totals[1] + second_piece)]
    reduce_sum x10 -> x0, other arithmetic: 11.2 us -> none  [the longest x1 3.51 us: body(): jnp.sum(cot_wide[:, None, :] * result_pick, axis=2)]
  transfers between devices with their start and end apart: 6 -> 0, of which waited for: 4 -> 0; matrix products, arithmetic and copies ran while one was open for 23% -> 0% of each run, Pallas kernels for 0% -> 0%
where the time goes in v1:
time: 161 us
  Pallas kernels  151 us (94%)
  local copies, waits for them, and re-layouts  9.48 us (6%)
    pallas_call x1, Pallas kernels, body(): pl.pallas_call(kernel, out_shape=(shape((TOK, D), BF), shape((TOK, D), BF...  151 us
    unnamed x12, local copies, waits for them, and re-layouts  7.93 us

profile of v1, /device:TPU:1, one launch (start us, length us, event | category | flops | bytes accessed | tf_op | source)
XLA Modules:
  0.0 160.8 jit_solution(1064850356504357081)
XLA Ops:
  0.6 0.0 copy-start.2
  0.6 1.4 copy.13.gw
  2.1 0.0 copy-done.2
  2.1 0.7 copy.14.ids
  2.8 150.7 %shard_map.119 = (bf16[128,1280]{1,0:T(8,128)(2,1)}, bf16[128,1280]{1,0:T(8,128)(2,1)}, f32[128,2]{1,0:T(8,128)}, bf16[2,160,1280]{2,1,0:T(8,128)(2,1)}, bf16[2,160,1280]{2,1,0:T(8,128)(2,1)}) custom-call(bf16[128,1280]{1,0:T(8,128)(2,1)} %tok.1, bf16[128,1280]{1,0:T(8,128)(2,1)} %cot.1, f32[128,2]{1,0:T(8,128)} %copy.13.gw, s32[128,2]{1,0:T(8,128)} %copy.14.ids, ...), custom_call_target="tpu_custom_call" | custom-call | tf_op jit(solution)/shard_map/pallas_call | solution.py:367
  153.5 0.0 copy-start.1
  153.5 1.5 copy.15
  155.1 1.7 %copy.20 = bf16[128,1280]{1,0:T(8,128)(2,1)} copy(bf16[128,1280]{1,0:T(8,128)(2,1)} %get-tuple-element.15) | data formatting | bytes 655360
  156.8 1.7 %copy.21 = bf16[128,1280]{1,0:T(8,128)(2,1)} copy(bf16[128,1280]{1,0:T(8,128)(2,1)} %get-tuple-element.16) | data formatting | bytes 655360
  158.5 0.0 copy-done.1
  158.5 0.0 copy-start
  158.5 0.9 copy.22
  159.4 0.5 copy-done
  160.0 0.9 copy.23
Async XLA Ops:
  0.6 1.4 copy-start.2
  153.5 5.0 %copy-start.1 = (bf16[2,160,1280]{2,1,0:T(8,128)(2,1)S(1)}, bf16[2,160,1280]{2,1,0:T(8,128)(2,1)}, u32[]{:S(2)}) copy-start(bf16[2,160,1280]{2,1,0:T(8,128)(2,1)} %get-tuple-element.18) | copy-start | bytes 2457604
  158.5 1.4 copy-start

commit v2 on v1

v2 whole, which is shorter than its diff:
```python
import jax
import jax.numpy as jnp
from jax import lax
from jax.experimental import pallas as pl
from jax.experimental.pallas import tpu as pltpu
from jax.sharding import PartitionSpec as P

MESH = pl.DeviceIdType.MESH
epsilon = 1e-06
root_half = 0.7071067811865476
density_scale = 0.3989422804014327

D = 1280
TOK = 128
SLOTS = 256
CAP = 16
NE = 16
SH = 160
HS = SH // 2
Q = 4 * HS
HID = 4 * Q
ROWS = 2 * SLOTS
ORDER = (0, 1, 3, 2)
SPANS = ((0, 3), (3, 5))
BF = jnp.bfloat16
F32 = jnp.float32


def dot(a, b, ca, cb):
    return lax.dot_general(a, b, (((ca,), (cb,)), ((), ())), preferred_element_type=F32)


def kernel(
    tok, cot, gw, ids, seg, keep, w1_in, w2_in,
    out, tg, gg, eg, rg,
    pt, normed, inv, wcol, acol, xs, gs, x_all, g_all, w1, w2, hid, slope, dpre, trans,
    y_send, y_recv, y_fin, y_ret, d_send, d_recv, d_fin, d_ret,
    e_own, e_send, e_core, e_wp, e_far, e_fin, r_own, r_send, r_core, r_wp, r_far, r_fin,
    a_ss, a_rs, b_ss, b_rs, p_ss, p_rs, q_ss, q_rs, w_ss, w_rs, wy_ss, wy_rs, wc_ss, wc_rs,
    gc_ss, gc_rs, gy_ss, gy_rs, gx_ss, gx_rs,
):
    dp = lax.axis_index("dp")
    ex = lax.axis_index("expert")
    y, x = dp // 4, dp % 4
    z, c = ex // 2, ex % 2
    row_mate = y + 1 - 2 * (y % 2)
    wgt_mate = (y + 5 - 2 * ((y + 1) % 2)) % 4
    other = 1 - c

    def dev(yy, xx, zz, cc):
        return (yy * 4 + xx, zz * 2 + cc)

    row_dev = dev(row_mate, x, z, c)
    wgt_dev = dev(wgt_mate, x, z, c)
    core_dev = dev(y, x, z, other)

    def remote(src, dst, ss, rs, target):
        return pltpu.make_async_remote_copy(
            src_ref=src, dst_ref=dst, send_sem=ss, recv_sem=rs, device_id=target, device_id_type=MESH
        )

    def arrived(dst, rs):
        pltpu.make_async_copy(dst, dst, rs).wait()

    def part(i, n):
        return pl.ds(pl.multiple_of(i * n, n), n)

    barrier = pltpu.get_barrier_semaphore()
    for dz in range(4):
        for dx in range(4):
            if dz or dx:
                pl.semaphore_signal(
                    barrier, inc=1, device_id=dev(y, (x + dx) % 4, (z + dz) % 4, c), device_id_type=MESH
                )
    for i in range(4):
        pl.semaphore_signal(barrier, inc=1, device_id=dev(y, i, z, other), device_id_type=MESH)
    for target in (row_dev, wgt_dev):
        pl.semaphore_signal(barrier, inc=1, device_id=target, device_id_type=MESH)
    pl.semaphore_wait(barrier, NE - 1 + 4 + 2)

    def weights_x(m, w_in, w, act):
        for l in range(2):
            for h in range(2):
                tx = 2 * c + l
                src = w_in.at[l, pl.ds(HS * h, HS)]
                dst = w.at[part(x, HS)]
                own = jnp.logical_and(tx == x, h == c)

                @pl.when(own)
                def _():
                    if act == "start":
                        pltpu.make_async_copy(src, dst, w_rs.at[m, x]).start()

                @pl.when(jnp.logical_not(own))
                def _():
                    copy = remote(src, dst, w_ss.at[m, 2 * l + h], w_rs.at[m, x], dev(y, tx, z, h))
                    copy.start() if act == "start" else copy.wait_send()

    weights_x(0, w1_in, w1, "start")

    def swap_blocks(src, dst, cols, ss, rs, act):
        mine = part(z * 4 + x, CAP)
        for dz in ORDER:
            for dx in ORDER:
                i = dz * 4 + dx
                tx, tz = (x + dx) % 4, (z + dz) % 4
                theirs = part(tz * 4 + tx, CAP)
                if i == 0:
                    if act == "start":
                        pltpu.make_async_copy(src.at[mine, cols], dst.at[mine, cols], rs.at[0]).start()
                else:
                    copy = remote(
                        src.at[theirs, cols], dst.at[mine, cols], ss.at[i], rs.at[i], dev(y, tx, tz, c)
                    )
                    copy.start() if act == "start" else copy.wait_send()

    def swap_wait(dst, cols, rs, dz):
        for dx in range(4):
            block = ((z + 4 - dz) % 4) * 4 + (x + 4 - dx) % 4
            arrived(dst.at[part(block, CAP), cols], rs.at[dz * 4 + dx])

    lane = lax.broadcasted_iota(jnp.int32, (TOK, TOK), 1)
    sub = lax.broadcasted_iota(jnp.int32, (TOK, TOK), 0)

    def column(row):
        wide_row = jnp.broadcast_to(row.astype(F32), (TOK, TOK))
        return jnp.sum(jnp.where(lane == sub, wide_row, 0.0), axis=1, keepdims=True)

    seg_row = jnp.broadcast_to(seg[...].astype(F32), (TOK, TOK))
    seg_col = column(seg[...])
    earlier = jnp.sum((seg_row < seg_col).astype(F32), axis=1, keepdims=True)
    images = keep.shape[1]
    image = lax.broadcasted_iota(jnp.int32, (TOK, images), 1).astype(F32)
    kept = jnp.broadcast_to(keep[...].astype(F32), (TOK, images))
    keep_token = jnp.sum(jnp.where(image == seg_col, kept, 0.0), axis=1, keepdims=True)
    position = lax.broadcasted_iota(jnp.int32, (TOK, 1), 0).astype(F32)
    alive = (position - earlier < keep_token).astype(F32)
    acol[...] = alive
    expert = lax.broadcasted_iota(jnp.int32, (TOK, NE), 1).astype(F32)
    chosen = [column(ids[k : k + 1, :]) for k in range(2)]
    match = [(chosen[k] == expert).astype(F32) for k in range(2)]
    before = dot((lane < sub).astype(BF), (match[0] + match[1]).astype(BF), 1, 0)
    slot_iota = lax.broadcasted_iota(jnp.int32, (TOK, SLOTS), 1).astype(F32)
    for k in range(2):
        wcol[:, k : k + 1] = column(gw[k : k + 1, :]) * alive
        slot = jnp.sum(before * match[k], axis=1, keepdims=True)
        if k == 1:
            slot = slot + jnp.sum(match[0] * match[1], axis=1, keepdims=True)
        pt[k] = (slot_iota == chosen[k] * CAP + slot).astype(BF)

    every = pl.ds(0, D)
    wide = tok[...].astype(F32)
    centred = wide - jnp.mean(wide, axis=1, keepdims=True)
    scale = lax.rsqrt(jnp.mean(centred * centred, axis=1, keepdims=True) + epsilon)
    inv[...] = scale
    normed[...] = centred * scale
    feats = (normed[...].astype(BF).astype(F32) * alive).astype(BF)
    xs[...] = dot(pt[0] + pt[1], feats, 0, 0).astype(BF)
    swap_blocks(xs, x_all, every, a_ss.at[0], a_rs.at[0], "start")
    grads = [(cot[...].astype(F32) * wcol[:, k : k + 1]).astype(BF) for k in range(2)]
    gs[...] = (dot(pt[0], grads[0], 0, 0) + dot(pt[1], grads[1], 0, 0)).astype(BF)
    swap_blocks(gs, g_all, every, a_ss.at[1], a_rs.at[1], "start")
    weights_x(1, w2_in, w2, "start")

    own_rows, mate_rows = pl.ds(0, SLOTS), pl.ds(SLOTS, SLOTS)
    group = 4 * CAP

    def rows_y(k, ref, g):
        src = ref.at[part(g, group)]
        dst = ref.at[part(g + SLOTS // group, group)]
        return remote(src, dst, b_ss.at[k, g], b_rs.at[k, g], row_dev)

    def rows_on(k, ref):
        for dz in ORDER:
            swap_wait(ref, every, a_rs.at[k], dz)
            rows_y(k, ref, (z + 4 - dz) % 4).start()

    def piece(w, s, h, i):
        return w.at[part((2 * s + h) * 4 + i, HS)]

    def weights_y(m, w, i):
        return remote(piece(w, 0, 0, i), piece(w, 1, 0, i), wy_ss.at[m, i], wy_rs.at[m, i], wgt_dev)

    def weights_core(m, w, s, i):
        return remote(piece(w, s, 0, i), piece(w, s, 1, i), wc_ss.at[m, s, i], wc_rs.at[m, s, i], core_dev)

    def weights_mid(m, w):
        for dx in ORDER:
            i = (x + dx) % 4
            arrived(w.at[part(i, HS)], w_rs.at[m, i])
            weights_y(m, w, i).start()
            weights_core(m, w, 0, i).start()

    def weights_last(m, w):
        for dx in ORDER:
            i = (x + dx) % 4
            weights_y(m, w, i).wait_recv()
            weights_core(m, w, 1, i).start()

    def weights_here(m, w):
        for s in range(2):
            for i in range(4):
                weights_core(m, w, s, i).wait_recv()

    weights_mid(0, w1)
    rows_on(0, x_all)
    weights_mid(1, w2)
    rows_on(1, g_all)
    weights_last(0, w1)
    for g in range(4):
        rows_y(0, x_all, g).wait_recv()
    weights_here(0, w1)

    def tile(j, n=256):
        return pl.ds(pl.multiple_of(j * n, n), n)

    @pl.loop(0, HID // 256)
    def _(j):
        pre = dot(x_all[...], w1[tile(j), :], 1, 1)
        cdf = 0.5 * (1.0 + lax.erf(pre * root_half))
        value = (pre * cdf).astype(BF)
        hid[:, tile(j)] = value
        trans[tile(j), :] = value.T
        slope[:, tile(j)] = cdf + pre * jnp.exp(-0.5 * pre * pre) * density_scale

    weights_last(1, w2)
    for g in range(4):
        rows_y(1, g_all, g).wait_recv()

    def grads_core(m, send, core, s, n):
        return remote(
            send.at[s, :, tile(n)], core.at[s, :, tile(n)], gc_ss.at[m, s, n], gc_rs.at[m, s, n], core_dev
        )

    def grads_y(m, wp, far, n):
        return remote(wp.at[:, tile(n)], far.at[:, tile(n)], gy_ss.at[m, n], gy_rs.at[m, n], wgt_dev)

    def grads_tile(m, right, own, send, core, s, n):
        sums = dot(trans[pl.ds(s * 2 * Q, 2 * Q), :], right[:, tile(n)], 1, 0)
        own[s, :, tile(n)] = sums[:Q]
        send[s, :, tile(n)] = sums[Q:].astype(BF)
        grads_core(m, send, core, s, n).start()

    def weight_grads(m, right, own, send, core, wp, far):
        @pl.loop(0, D // 256)
        def _(n):
            grads_tile(m, right, own, send, core, 1, n)

        @pl.loop(0, D // 256)
        def _(n):
            grads_core(m, send, core, 1, n).wait_recv()
            wp[:, tile(n)] = (own[1, :, tile(n)] + core[1, :, tile(n)].astype(F32)).astype(BF)
            grads_y(m, wp, far, n).start()
            grads_tile(m, right, own, send, core, 0, n)

    def grads_x(m, fin, result, n, act):
        for i in range(4):
            src = fin.at[pl.ds(i * HS, HS), tile(n)]
            dst = result.at[x % 2, part(c, HS), tile(n)]
            rs = gx_rs.at[m, n, 2 * (x % 2) + c]
            own = jnp.logical_and(i == x, c == x // 2)

            @pl.when(own)
            def _():
                if act == "start":
                    pltpu.make_async_copy(src, dst, rs).start()

            @pl.when(jnp.logical_not(own))
            def _():
                copy = remote(src, dst, gx_ss.at[m, n, i], rs, dev(y, i, z, x // 2))
                copy.start() if act == "start" else copy.wait_send()

    def grads_last(m, own, send, core, wp, far, fin, result):
        @pl.loop(0, D // 256)
        def _(n):
            grads_core(m, send, core, 0, n).wait_recv()
            grads_y(m, wp, far, n).wait_recv()
            sums = own[0, :, tile(n)] + core[0, :, tile(n)].astype(F32) + far[:, tile(n)].astype(F32)
            fin[:, tile(n)] = sums.astype(BF)
            grads_x(m, fin, result, n, "start")

    def sums_y(k, send, recv, n):
        return remote(send.at[:, tile(n)], recv.at[:, tile(n)], p_ss.at[k, n], p_rs.at[k, n], row_dev)

    def results_mate(k, left, w, send, recv):
        @pl.loop(0, D // 256)
        def _(n):
            send[:, tile(n)] = dot(left[mate_rows, :], w[:, tile(n)], 1, 0).astype(BF)
            sums_y(k, send, recv, n).start()

    def results_own(k, left, w, send, recv, fin, ret):
        for h, (low, high) in enumerate(SPANS):

            @pl.loop(low, high)
            def _(n):
                own = dot(left[own_rows, :], w[:, tile(n)], 1, 0)
                sums_y(k, send, recv, n).wait_recv()
                fin[:, tile(n)] = (own + recv[:, tile(n)].astype(F32)).astype(BF)

            swap_blocks(fin, ret, span(h), q_ss.at[k, h], q_rs.at[k, h], "start")

    def span(h):
        return pl.ds(SPANS[h][0] * 256, (SPANS[h][1] - SPANS[h][0]) * 256)

    weight_grads(1, g_all, r_own, r_send, r_core, r_wp, r_far)
    weights_here(1, w2)
    results_mate(0, hid, w2, y_send, y_recv)

    @pl.loop(0, HID // 256)
    def _(j):
        back = dot(g_all[...], w2[tile(j), :], 1, 1)
        value = (back * slope[:, tile(j)]).astype(BF)
        dpre[:, tile(j)] = value
        trans[tile(j), :] = value.T

    results_mate(1, dpre, w1, d_send, d_recv)
    weight_grads(0, x_all, e_own, e_send, e_core, e_wp, e_far)
    results_own(0, hid, w2, y_send, y_recv, y_fin, y_ret)
    grads_last(1, r_own, r_send, r_core, r_wp, r_far, r_fin, rg)
    results_own(1, dpre, w1, d_send, d_recv, d_fin, d_ret)

    for h in range(len(SPANS)):
        for dz in range(4):
            swap_wait(y_ret, span(h), q_rs.at[0, h], dz)
    result = tok[...].astype(F32)
    for k in range(2):
        pick = dot(pt[k], y_ret[...], 1, 0)
        result = result + pick * wcol[:, k : k + 1]
        inner = acol[...] * jnp.sum(cot[...].astype(F32) * pick, axis=1, keepdims=True)
        gg[k : k + 1, :] = jnp.sum(jnp.where(lane == sub, inner, 0.0), axis=0, keepdims=True)
    out[...] = result.astype(BF)
    for h in range(len(SPANS)):
        for dz in range(4):
            swap_wait(d_ret, span(h), q_rs.at[1, h], dz)
    dnorm = (dot(pt[0], d_ret[...], 1, 0) + dot(pt[1], d_ret[...], 1, 0)) * acol[...]
    tail = dnorm - jnp.mean(dnorm, axis=1, keepdims=True)
    tail = tail - normed[...] * jnp.mean(dnorm * normed[...], axis=1, keepdims=True)
    tg[...] = (cot[...].astype(F32) + inv[...] * tail).astype(BF)

    grads_last(0, e_own, e_send, e_core, e_wp, e_far, e_fin, eg)

    for m, result in ((1, rg), (0, eg)):

        @pl.loop(0, D // 256)
        def _(n):
            for l in range(2):
                for h in range(2):
                    arrived(result.at[l, pl.ds(h * HS, HS), tile(n)], gx_rs.at[m, n, 2 * l + h])

    for m, (w_in, w) in enumerate(((w1_in, w1), (w2_in, w2))):
        weights_x(m, w_in, w, "wait")
        for i in range(4):
            weights_y(m, w, i).wait_send()
            for s in range(2):
                weights_core(m, w, s, i).wait_send()
    for k, (src, dst) in enumerate(((xs, x_all), (gs, g_all))):
        swap_blocks(src, dst, every, a_ss.at[k], a_rs.at[k], "wait")
        for g in range(4):
            rows_y(k, dst, g).wait_send()
    for k, (send, recv, fin, ret) in enumerate(((y_send, y_recv, y_fin, y_ret), (d_send, d_recv, d_fin, d_ret))):
        for h in range(len(SPANS)):
            swap_blocks(fin, ret, span(h), q_ss.at[k, h], q_rs.at[k, h], "wait")

        @pl.loop(0, D // 256)
        def _(n):
            sums_y(k, send, recv, n).wait_send()

    for m, send, core, wp, far, fin, result in (
        (0, e_send, e_core, e_wp, e_far, e_fin, eg),
        (1, r_send, r_core, r_wp, r_far, r_fin, rg),
    ):

        @pl.loop(0, D // 256)
        def _(n):
            for s in range(2):
                grads_core(m, send, core, s, n).wait_send()
            grads_y(m, wp, far, n).wait_send()
            grads_x(m, fin, result, n, "wait")


def hand_out(*refs):
    sems = refs[-1]
    half = len(refs) // 2
    copies = [pltpu.make_async_copy(refs[i], refs[half + i], sems.at[i]) for i in range(half)]
    for copy in copies:
        copy.start()
    for copy in copies:
        copy.wait()


def body(tokens, cotangent, gate_weights, expert_ids, *rest):
    vmem = pl.BlockSpec(memory_space=pltpu.VMEM)
    hbm = pl.BlockSpec(memory_space=pl.ANY)
    dma = pltpu.SemaphoreType.DMA
    shape = jax.ShapeDtypeStruct
    tiles = D // 256
    grad_scratch = [
        pltpu.VMEM((2, Q, D), F32),
        pltpu.VMEM((2, Q, D), BF),
        pltpu.VMEM((2, Q, D), BF),
        pltpu.VMEM((Q, D), BF),
        pltpu.VMEM((Q, D), BF),
        pltpu.VMEM((Q, D), BF),
    ]
    shapes = (
        shape((TOK, D), BF),
        shape((TOK, D), BF),
        shape((2, TOK), F32),
        shape((2, SH, D), BF),
        shape((2, SH, D), BF),
    )
    results = pl.pallas_call(
        kernel,
        out_shape=shapes,
        in_specs=[vmem] * 6 + [hbm] * 2,
        out_specs=(vmem, vmem, vmem, hbm, hbm),
        scratch_shapes=[
            pltpu.VMEM((2, TOK, SLOTS), BF),
            pltpu.VMEM((TOK, D), F32),
            pltpu.VMEM((TOK, 1), F32),
            pltpu.VMEM((TOK, 2), F32),
            pltpu.VMEM((TOK, 1), F32),
            pltpu.VMEM((SLOTS, D), BF),
            pltpu.VMEM((SLOTS, D), BF),
            pltpu.VMEM((ROWS, D), BF),
            pltpu.VMEM((ROWS, D), BF),
            pltpu.VMEM((HID, D), BF),
            pltpu.VMEM((HID, D), BF),
            pltpu.VMEM((ROWS, HID), BF),
            pltpu.VMEM((ROWS, HID), F32),
            pltpu.VMEM((ROWS, HID), BF),
            pltpu.VMEM((HID, ROWS), BF),
        ]
        + [pltpu.VMEM((SLOTS, D), BF)] * 8
        + grad_scratch * 2
        + [
            dma((2, NE)),
            dma((2, NE)),
            dma((2, 4)),
            dma((2, 4)),
            dma((2, tiles)),
            dma((2, tiles)),
            dma((2, len(SPANS), NE)),
            dma((2, len(SPANS), NE)),
            dma((2, 4)),
            dma((2, 4)),
            dma((2, 4)),
            dma((2, 4)),
            dma((2, 2, 4)),
            dma((2, 2, 4)),
            dma((2, 2, tiles)),
            dma((2, 2, tiles)),
            dma((2, tiles)),
            dma((2, tiles)),
            dma((2, tiles, 4)),
            dma((2, tiles, 4)),
        ],
        compiler_params=pltpu.CompilerParams(
            collective_id=0, has_side_effects=True, vmem_limit_bytes=60 * 2**20
        ),
    )(tokens, cotangent, gate_weights.T, expert_ids.T, *rest)
    out, tg, gg, eg, rg = pl.pallas_call(
        hand_out,
        out_shape=shapes,
        in_specs=[hbm] * 5,
        out_specs=(hbm,) * 5,
        scratch_shapes=[dma((5,))],
    )(*results)
    return out, tg, gg.T, eg, rg


def solution(mesh):
    rows = P(("dp", "expert"), None)
    weights = P("expert", "dp", None)
    return jax.shard_map(
        body,
        mesh=mesh,
        in_specs=(rows,) * 6 + (weights,) * 2,
        out_specs=(rows,) * 3 + (weights,) * 2,
        check_vma=False,
    )
```

time: 161 us -> 187 us (1.16)
  Pallas kernels: 151 us -> 186 us
  local copies, waits for them, and re-layouts: 9.48 us -> 0 us
    pallas_call x1 -> x2, Pallas kernels: 151 us -> 186 us  [the longest x1 115 us: body(): pl.pallas_call(kernel, out_shape=shapes, in_specs=[vmem] * 6 + [hbm] * 2,...]
    unnamed x12 -> x0, local copies, waits for them, and re-layouts: 7.93 us -> none
where the time goes in v2:
time: 187 us; the launch traced here: 186 us
  Pallas kernels  186 us (99%)
    pallas_call x1, Pallas kernels, body(): pl.pallas_call(kernel, out_shape=shapes, in_specs=[vmem] * 6 + [hbm] * 2,...  115 us
    pallas_call x1, Pallas kernels, body(): pl.pallas_call(hand_out, out_shape=shapes, in_specs=[hbm] * 5, out_specs=...  70.7 us

profile of v2, /device:TPU:1, one launch (start us, length us, event | category | flops | bytes accessed | tf_op | source)
XLA Modules:
  0.0 186.5 jit_solution(9307971226824620131)
XLA Ops:
  0.6 115.2 %shard_map.119 = (bf16[128,1280]{1,0:T(8,128)(2,1)}, bf16[128,1280]{1,0:T(8,128)(2,1)}, f32[2,128]{1,0:T(2,128)}, bf16[2,160,1280]{2,1,0:T(8,128)(2,1)}, bf16[2,160,1280]{2,1,0:T(8,128)(2,1)}) custom-call(bf16[128,1280]{1,0:T(8,128)(2,1)} %tok.1, bf16[128,1280]{1,0:T(8,128)(2,1)} %cot.1, f32[2,128]{1,0:T(2,128)} %bitcast.3, s32[2,128]{1,0:T(2,128)} %bitcast.4, ...), custom_call_target="tpu_custom_call" | custom-call | tf_op jit(solution)/shard_map/pallas_call | solution.py:412
  115.8 70.7 %shard_map.120 = (bf16[128,1280]{1,0:T(8,128)(2,1)}, bf16[128,1280]{1,0:T(8,128)(2,1)}, f32[2,128]{1,0:T(2,128)}, bf16[2,160,1280]{2,1,0:T(8,128)(2,1)}, bf16[2,160,1280]{2,1,0:T(8,128)(2,1)}) custom-call(bf16[128,1280]{1,0:T(8,128)(2,1)} %get-tuple-element.15.refs_0_, bf16[128,1280]{1,0:T(8,128)(2,1)} %get-tuple-element.16.refs_1_, ...), custom_call_target="tpu_custom_call" | custom-call | tf_op jit(solution)/shard_map/pallas_call | solution.py:462

commit v3 on v2

--- a/solution.py
+++ b/solution.py
@@ -76,7 +76,6 @@
         pl.semaphore_signal(barrier, inc=1, device_id=dev(y, i, z, other), device_id_type=MESH)
     for target in (row_dev, wgt_dev):
         pl.semaphore_signal(barrier, inc=1, device_id=target, device_id_type=MESH)
-    pl.semaphore_wait(barrier, NE - 1 + 4 + 2)
 
     def weights_x(m, w_in, w, act):
         for l in range(2):
@@ -95,8 +94,6 @@
                 def _():
                     copy = remote(src, dst, w_ss.at[m, 2 * l + h], w_rs.at[m, x], dev(y, tx, z, h))
                     copy.start() if act == "start" else copy.wait_send()
-
-    weights_x(0, w1_in, w1, "start")
 
     def swap_blocks(src, dst, cols, ss, rs, act):
         mine = part(z * 4 + x, CAP)
@@ -156,6 +153,9 @@
     normed[...] = centred * scale
     feats = (normed[...].astype(BF).astype(F32) * alive).astype(BF)
     xs[...] = dot(pt[0] + pt[1], feats, 0, 0).astype(BF)
+
+    pl.semaphore_wait(barrier, NE - 1 + 4 + 2)
+    weights_x(0, w1_in, w1, "start")
     swap_blocks(xs, x_all, every, a_ss.at[0], a_rs.at[0], "start")
     grads = [(cot[...].astype(F32) * wcol[:, k : k + 1]).astype(BF) for k in range(2)]
     gs[...] = (dot(pt[0], grads[0], 0, 0) + dot(pt[1], grads[1], 0, 0)).astype(BF)
@@ -463,7 +463,7 @@
         hand_out,
         out_shape=shapes,
         in_specs=[hbm] * 5,
-        out_specs=(hbm,) * 5,
+        out_specs=(vmem,) * 5,
         scratch_shapes=[dma((5,))],
     )(*results)
     return out, tg, gg.T, eg, rg

time: 187 us -> 118 us (0.63)
  Pallas kernels: 186 us -> 117 us
    pallas_call x1, Pallas kernels: 70.7 us -> 3.02 us  [body(): pl.pallas_call(hand_out, out_shape=shapes, in_specs=[hbm] * 5, out_specs=...]
where the time goes in v3:
time: 118 us
  Pallas kernels  117 us (99%)
    pallas_call x1, Pallas kernels, body(): pl.pallas_call(kernel, out_shape=shapes, in_specs=[vmem] * 6 + [hbm] * 2,...  114 us
    pallas_call x1, Pallas kernels, body(): pl.pallas_call(hand_out, out_shape=shapes, in_specs=[hbm] * 5, out_specs=...  3.02 us

profile of v3, /device:TPU:1, one launch (start us, length us, event | category | flops | bytes accessed | tf_op | source)
XLA Modules:
  0.0 117.6 jit_solution(3106448270839750865)
XLA Ops:
  0.6 113.9 %shard_map.119 = (bf16[128,1280]{1,0:T(8,128)(2,1)}, bf16[128,1280]{1,0:T(8,128)(2,1)}, f32[2,128]{1,0:T(2,128)}, bf16[2,160,1280]{2,1,0:T(8,128)(2,1)}, bf16[2,160,1280]{2,1,0:T(8,128)(2,1)}) custom-call(bf16[128,1280]{1,0:T(8,128)(2,1)} %tok.1, bf16[128,1280]{1,0:T(8,128)(2,1)} %cot.1, f32[2,128]{1,0:T(2,128)} %bitcast.3, s32[2,128]{1,0:T(2,128)} %bitcast.4, ...), custom_call_target="tpu_custom_call" | custom-call | tf_op jit(solution)/shard_map/pallas_call | solution.py:412
  114.6 3.0 %shard_map.120 = (bf16[128,1280]{1,0:T(8,128)(2,1)}, bf16[128,1280]{1,0:T(8,128)(2,1)}, f32[2,128]{1,0:T(2,128)}, bf16[2,160,1280]{2,1,0:T(8,128)(2,1)}, bf16[2,160,1280]{2,1,0:T(8,128)(2,1)}) custom-call(bf16[128,1280]{1,0:T(8,128)(2,1)} %get-tuple-element.15.refs_0_, bf16[128,1280]{1,0:T(8,128)(2,1)} %get-tuple-element.16.refs_1_, ...), custom_call_target="tpu_custom_call" | custom-call | tf_op jit(solution)/shard_map/pallas_call | solution.py:462

commit v4 on v3

--- a/solution.py
+++ b/solution.py
@@ -156,11 +156,8 @@
 
     pl.semaphore_wait(barrier, NE - 1 + 4 + 2)
     weights_x(0, w1_in, w1, "start")
-    swap_blocks(xs, x_all, every, a_ss.at[0], a_rs.at[0], "start")
     grads = [(cot[...].astype(F32) * wcol[:, k : k + 1]).astype(BF) for k in range(2)]
     gs[...] = (dot(pt[0], grads[0], 0, 0) + dot(pt[1], grads[1], 0, 0)).astype(BF)
-    swap_blocks(gs, g_all, every, a_ss.at[1], a_rs.at[1], "start")
-    weights_x(1, w2_in, w2, "start")
 
     own_rows, mate_rows = pl.ds(0, SLOTS), pl.ds(SLOTS, SLOTS)
     group = 4 * CAP
@@ -170,10 +167,9 @@
         dst = ref.at[part(g + SLOTS // group, group)]
         return remote(src, dst, b_ss.at[k, g], b_rs.at[k, g], row_dev)
 
-    def rows_on(k, ref):
-        for dz in ORDER:
-            swap_wait(ref, every, a_rs.at[k], dz)
-            rows_y(k, ref, (z + 4 - dz) % 4).start()
+    def rows_on(k, ref, dz):
+        swap_wait(ref, every, a_rs.at[k], dz)
+        rows_y(k, ref, (z + 4 - dz) % 4).start()
 
     def piece(w, s, h, i):
         return w.at[part((2 * s + h) * 4 + i, HS)]
@@ -184,12 +180,11 @@
     def weights_core(m, w, s, i):
         return remote(piece(w, s, 0, i), piece(w, s, 1, i), wc_ss.at[m, s, i], wc_rs.at[m, s, i], core_dev)
 
-    def weights_mid(m, w):
-        for dx in ORDER:
-            i = (x + dx) % 4
-            arrived(w.at[part(i, HS)], w_rs.at[m, i])
-            weights_y(m, w, i).start()
-            weights_core(m, w, 0, i).start()
+    def weights_on(m, w, dx):
+        i = (x + dx) % 4
+        arrived(w.at[part(i, HS)], w_rs.at[m, i])
+        weights_y(m, w, i).start()
+        weights_core(m, w, 0, i).start()
 
     def weights_last(m, w):
         for dx in ORDER:
@@ -202,10 +197,26 @@
             for i in range(4):
                 weights_core(m, w, s, i).wait_recv()
 
-    weights_mid(0, w1)
-    rows_on(0, x_all)
-    weights_mid(1, w2)
-    rows_on(1, g_all)
+    first_w = (lambda: weights_x(0, w1_in, w1, "start"), lambda dx: weights_on(0, w1, dx))
+    second_w = (lambda: weights_x(1, w2_in, w2, "start"), lambda dx: weights_on(1, w2, dx))
+    first_r = (
+        lambda: swap_blocks(xs, x_all, every, a_ss.at[0], a_rs.at[0], "start"),
+        lambda dz: rows_on(0, x_all, dz),
+    )
+    second_r = (
+        lambda: swap_blocks(gs, g_all, every, a_ss.at[1], a_rs.at[1], "start"),
+        lambda dz: rows_on(1, g_all, dz),
+    )
+    STAGES = (first_w, first_r, second_r, second_w)
+    for begin, _ in STAGES[1:2]:
+        begin()
+    for stage, (_, land) in enumerate(STAGES):
+        for dd in ORDER[:3]:
+            land(dd)
+        if stage + 2 < len(STAGES):
+            STAGES[stage + 2][0]()
+        for dd in ORDER[3:]:
+            land(dd)
     weights_last(0, w1)
     for g in range(4):
         rows_y(0, x_all, g).wait_recv()
@@ -223,7 +234,6 @@
         trans[tile(j), :] = value.T
         slope[:, tile(j)] = cdf + pre * jnp.exp(-0.5 * pre * pre) * density_scale
 
-    weights_last(1, w2)
     for g in range(4):
         rows_y(1, g_all, g).wait_recv()
 
@@ -303,9 +313,9 @@
         return pl.ds(SPANS[h][0] * 256, (SPANS[h][1] - SPANS[h][0]) * 256)
 
     weight_grads(1, g_all, r_own, r_send, r_core, r_wp, r_far)
+    weights_last(1, w2)
     weights_here(1, w2)
     results_mate(0, hid, w2, y_send, y_recv)
-
     @pl.loop(0, HID // 256)
     def _(j):
         back = dot(g_all[...], w2[tile(j), :], 1, 1)
@@ -315,10 +325,10 @@
 
     results_mate(1, dpre, w1, d_send, d_recv)
     weight_grads(0, x_all, e_own, e_send, e_core, e_wp, e_far)
+    grads_last(1, r_own, r_send, r_core, r_wp, r_far, r_fin, rg)
     results_own(0, hid, w2, y_send, y_recv, y_fin, y_ret)
-    grads_last(1, r_own, r_send, r_core, r_wp, r_far, r_fin, rg)
     results_own(1, dpre, w1, d_send, d_recv, d_fin, d_ret)
-
+    grads_last(0, e_own, e_send, e_core, e_wp, e_far, e_fin, eg)
     for h in range(len(SPANS)):
         for dz in range(4):
             swap_wait(y_ret, span(h), q_rs.at[0, h], dz)
@@ -337,7 +347,6 @@
     tail = tail - normed[...] * jnp.mean(dnorm * normed[...], axis=1, keepdims=True)
     tg[...] = (cot[...].astype(F32) + inv[...] * tail).astype(BF)
 
-    grads_last(0, e_own, e_send, e_core, e_wp, e_far, e_fin, eg)
 
     for m, result in ((1, rg), (0, eg)):
 

time: 118 us -> 113 us (0.958)
  Pallas kernels: 117 us -> 112 us
    pallas_call x1, Pallas kernels: 114 us -> 109 us  [body(): pl.pallas_call(kernel, out_shape=shapes, in_specs=[vmem] * 6 + [hbm] * 2,...]
where the time goes in v4:
time: 113 us
  Pallas kernels  112 us (99%)
    pallas_call x1, Pallas kernels, body(): pl.pallas_call(kernel, out_shape=shapes, in_specs=[vmem] * 6 + [hbm] * 2,...  109 us
    pallas_call x1, Pallas kernels, body(): pl.pallas_call(hand_out, out_shape=shapes, in_specs=[hbm] * 5, out_specs=...  3.02 us

profile of v4, /device:TPU:1, one launch (start us, length us, event | category | flops | bytes accessed | tf_op | source)
XLA Modules:
  0.0 112.7 jit_solution(17291796329629257192)
XLA Ops:
  0.6 109.0 %shard_map.119 = (bf16[128,1280]{1,0:T(8,128)(2,1)}, bf16[128,1280]{1,0:T(8,128)(2,1)}, f32[2,128]{1,0:T(2,128)}, bf16[2,160,1280]{2,1,0:T(8,128)(2,1)}, bf16[2,160,1280]{2,1,0:T(8,128)(2,1)}) custom-call(bf16[128,1280]{1,0:T(8,128)(2,1)} %tok.1, bf16[128,1280]{1,0:T(8,128)(2,1)} %cot.1, f32[2,128]{1,0:T(2,128)} %bitcast.3, s32[2,128]{1,0:T(2,128)} %bitcast.4, ...), custom_call_target="tpu_custom_call" | custom-call | tf_op jit(solution)/shard_map/pallas_call | solution.py:421
  109.6 3.0 %shard_map.120 = (bf16[128,1280]{1,0:T(8,128)(2,1)}, bf16[128,1280]{1,0:T(8,128)(2,1)}, f32[2,128]{1,0:T(2,128)}, bf16[2,160,1280]{2,1,0:T(8,128)(2,1)}, bf16[2,160,1280]{2,1,0:T(8,128)(2,1)}) custom-call(bf16[128,1280]{1,0:T(8,128)(2,1)} %get-tuple-element.15.refs_0_, bf16[128,1280]{1,0:T(8,128)(2,1)} %get-tuple-element.16.refs_1_, ...), custom_call_target="tpu_custom_call" | custom-call | tf_op jit(solution)/shard_map/pallas_call | solution.py:471

commit v5 on v3

--- a/solution.py
+++ b/solution.py
@@ -21,6 +21,18 @@
 HID = 4 * Q
 ROWS = 2 * SLOTS
 ORDER = (0, 1, 3, 2)
+STAGES = (
+    (0, 0, 0),
+    (0, 0, 1),
+    (0, 1, 0),
+    (0, 1, 1),
+    (1, 0, 0),
+    (1, 0, 1),
+    (1, 1, 0),
+    (1, 1, 1),
+)
+HEAD, FLIGHT, LEAD = 2, 3, 3
+CUTS = 2
 SPANS = ((0, 3), (3, 5))
 BF = jnp.bfloat16
 F32 = jnp.float32
@@ -77,22 +89,27 @@
     for target in (row_dev, wgt_dev):
         pl.semaphore_signal(barrier, inc=1, device_id=target, device_id_type=MESH)
 
-    def weights_x(m, w_in, w, act):
+    def cut(q):
+        return pl.ds(q * (D // CUTS), D // CUTS)
+
+    def weights_x(m, q, w_in, w, act):
         for l in range(2):
             for h in range(2):
                 tx = 2 * c + l
-                src = w_in.at[l, pl.ds(HS * h, HS)]
-                dst = w.at[part(x, HS)]
+                src = w_in.at[l, pl.ds(HS * h, HS), cut(q)]
+                dst = w.at[part(x, HS), cut(q)]
                 own = jnp.logical_and(tx == x, h == c)
 
                 @pl.when(own)
                 def _():
                     if act == "start":
-                        pltpu.make_async_copy(src, dst, w_rs.at[m, x]).start()
+                        pltpu.make_async_copy(src, dst, w_rs.at[m, q, x]).start()
 
                 @pl.when(jnp.logical_not(own))
                 def _():
-                    copy = remote(src, dst, w_ss.at[m, 2 * l + h], w_rs.at[m, x], dev(y, tx, z, h))
+                    copy = remote(
+                        src, dst, w_ss.at[m, q, 2 * l + h], w_rs.at[m, q, x], dev(y, tx, z, h)
+                    )
                     copy.start() if act == "start" else copy.wait_send()
 
     def swap_blocks(src, dst, cols, ss, rs, act):
@@ -115,6 +132,12 @@
         for dx in range(4):
             block = ((z + 4 - dz) % 4) * 4 + (x + 4 - dx) % 4
             arrived(dst.at[part(block, CAP), cols], rs.at[dz * 4 + dx])
+
+    def begin(m, q, rows):
+        if rows:
+            swap_blocks((xs, gs)[m], (x_all, g_all)[m], cut(q), a_ss.at[m, q], a_rs.at[m, q], "start")
+        else:
+            weights_x(m, q, (w1_in, w2_in)[m], (w1, w2)[m], "start")
 
     lane = lax.broadcasted_iota(jnp.int32, (TOK, TOK), 1)
     sub = lax.broadcasted_iota(jnp.int32, (TOK, TOK), 0)
@@ -145,7 +168,6 @@
             slot = slot + jnp.sum(match[0] * match[1], axis=1, keepdims=True)
         pt[k] = (slot_iota == chosen[k] * CAP + slot).astype(BF)
 
-    every = pl.ds(0, D)
     wide = tok[...].astype(F32)
     centred = wide - jnp.mean(wide, axis=1, keepdims=True)
     scale = lax.rsqrt(jnp.mean(centred * centred, axis=1, keepdims=True) + epsilon)
@@ -155,60 +177,74 @@
     xs[...] = dot(pt[0] + pt[1], feats, 0, 0).astype(BF)
 
     pl.semaphore_wait(barrier, NE - 1 + 4 + 2)
-    weights_x(0, w1_in, w1, "start")
-    swap_blocks(xs, x_all, every, a_ss.at[0], a_rs.at[0], "start")
+    for stage in STAGES[:HEAD]:
+        begin(*stage)
     grads = [(cot[...].astype(F32) * wcol[:, k : k + 1]).astype(BF) for k in range(2)]
     gs[...] = (dot(pt[0], grads[0], 0, 0) + dot(pt[1], grads[1], 0, 0)).astype(BF)
-    swap_blocks(gs, g_all, every, a_ss.at[1], a_rs.at[1], "start")
-    weights_x(1, w2_in, w2, "start")
 
     own_rows, mate_rows = pl.ds(0, SLOTS), pl.ds(SLOTS, SLOTS)
     group = 4 * CAP
 
-    def rows_y(k, ref, g):
-        src = ref.at[part(g, group)]
-        dst = ref.at[part(g + SLOTS // group, group)]
-        return remote(src, dst, b_ss.at[k, g], b_rs.at[k, g], row_dev)
-
-    def rows_on(k, ref):
-        for dz in ORDER:
-            swap_wait(ref, every, a_rs.at[k], dz)
-            rows_y(k, ref, (z + 4 - dz) % 4).start()
-
-    def piece(w, s, h, i):
-        return w.at[part((2 * s + h) * 4 + i, HS)]
-
-    def weights_y(m, w, i):
-        return remote(piece(w, 0, 0, i), piece(w, 1, 0, i), wy_ss.at[m, i], wy_rs.at[m, i], wgt_dev)
-
-    def weights_core(m, w, s, i):
-        return remote(piece(w, s, 0, i), piece(w, s, 1, i), wc_ss.at[m, s, i], wc_rs.at[m, s, i], core_dev)
-
-    def weights_mid(m, w):
-        for dx in ORDER:
-            i = (x + dx) % 4
-            arrived(w.at[part(i, HS)], w_rs.at[m, i])
-            weights_y(m, w, i).start()
-            weights_core(m, w, 0, i).start()
+    def rows_y(k, q, ref, g):
+        src = ref.at[part(g, group), cut(q)]
+        dst = ref.at[part(g + SLOTS // group, group), cut(q)]
+        return remote(src, dst, b_ss.at[k, q, g], b_rs.at[k, q, g], row_dev)
+
+    def rows_on(k, q, ref, dz):
+        swap_wait(ref, cut(q), a_rs.at[k, q], dz)
+        rows_y(k, q, ref, (z + 4 - dz) % 4).start()
+
+    def piece(w, q, s, h, i):
+        return w.at[part((2 * s + h) * 4 + i, HS), cut(q)]
+
+    def weights_y(m, q, w, i):
+        return remote(
+            piece(w, q, 0, 0, i), piece(w, q, 1, 0, i), wy_ss.at[m, q, i], wy_rs.at[m, q, i], wgt_dev
+        )
+
+    def weights_core(m, q, w, s, i):
+        return remote(
+            piece(w, q, s, 0, i), piece(w, q, s, 1, i), wc_ss.at[m, q, s, i], wc_rs.at[m, q, s, i], core_dev
+        )
+
+    def weights_on(m, q, w, dx):
+        i = (x + dx) % 4
+        arrived(w.at[part(i, HS), cut(q)], w_rs.at[m, q, i])
+        weights_y(m, q, w, i).start()
+        weights_core(m, q, w, 0, i).start()
 
     def weights_last(m, w):
-        for dx in ORDER:
-            i = (x + dx) % 4
-            weights_y(m, w, i).wait_recv()
-            weights_core(m, w, 1, i).start()
+        for q in range(CUTS):
+            for dx in ORDER:
+                i = (x + dx) % 4
+                weights_y(m, q, w, i).wait_recv()
+                weights_core(m, q, w, 1, i).start()
 
     def weights_here(m, w):
-        for s in range(2):
-            for i in range(4):
-                weights_core(m, w, s, i).wait_recv()
-
-    weights_mid(0, w1)
-    rows_on(0, x_all)
-    weights_mid(1, w2)
-    rows_on(1, g_all)
+        for q in range(CUTS):
+            for s in range(2):
+                for i in range(4):
+                    weights_core(m, q, w, s, i).wait_recv()
+
+    def land(m, q, rows, dd):
+        if rows:
+            rows_on(m, q, (x_all, g_all)[m], dd)
+        else:
+            weights_on(m, q, (w1, w2)[m], dd)
+
+    for stage in STAGES[HEAD:FLIGHT]:
+        begin(*stage)
+    for n, stage in enumerate(STAGES):
+        for dd in ORDER[:LEAD]:
+            land(*stage, dd)
+        if n + FLIGHT < len(STAGES):
+            begin(*STAGES[n + FLIGHT])
+        for dd in ORDER[LEAD:]:
+            land(*stage, dd)
     weights_last(0, w1)
-    for g in range(4):
-        rows_y(0, x_all, g).wait_recv()
+    for q in range(CUTS):
+        for g in range(4):
+            rows_y(0, q, x_all, g).wait_recv()
     weights_here(0, w1)
 
     def tile(j, n=256):
@@ -223,9 +259,6 @@
         trans[tile(j), :] = value.T
         slope[:, tile(j)] = cdf + pre * jnp.exp(-0.5 * pre * pre) * density_scale
 
-    weights_last(1, w2)
-    for g in range(4):
-        rows_y(1, g_all, g).wait_recv()
 
     def grads_core(m, send, core, s, n):
         return remote(
@@ -302,10 +335,13 @@
     def span(h):
         return pl.ds(SPANS[h][0] * 256, (SPANS[h][1] - SPANS[h][0]) * 256)
 
+    for q in range(CUTS):
+        for g in range(4):
+            rows_y(1, q, g_all, g).wait_recv()
+    weights_last(1, w2)
     weight_grads(1, g_all, r_own, r_send, r_core, r_wp, r_far)
     weights_here(1, w2)
     results_mate(0, hid, w2, y_send, y_recv)
-
     @pl.loop(0, HID // 256)
     def _(j):
         back = dot(g_all[...], w2[tile(j), :], 1, 1)
@@ -315,10 +351,10 @@
 
     results_mate(1, dpre, w1, d_send, d_recv)
     weight_grads(0, x_all, e_own, e_send, e_core, e_wp, e_far)
+    grads_last(1, r_own, r_send, r_core, r_wp, r_far, r_fin, rg)
     results_own(0, hid, w2, y_send, y_recv, y_fin, y_ret)
-    grads_last(1, r_own, r_send, r_core, r_wp, r_far, r_fin, rg)
     results_own(1, dpre, w1, d_send, d_recv, d_fin, d_ret)
-
+    grads_last(0, e_own, e_send, e_core, e_wp, e_far, e_fin, eg)
     for h in range(len(SPANS)):
         for dz in range(4):
             swap_wait(y_ret, span(h), q_rs.at[0, h], dz)
@@ -337,7 +373,6 @@
     tail = tail - normed[...] * jnp.mean(dnorm * normed[...], axis=1, keepdims=True)
     tg[...] = (cot[...].astype(F32) + inv[...] * tail).astype(BF)
 
-    grads_last(0, e_own, e_send, e_core, e_wp, e_far, e_fin, eg)
 
     for m, result in ((1, rg), (0, eg)):
 
@@ -348,15 +383,17 @@
                     arrived(result.at[l, pl.ds(h * HS, HS), tile(n)], gx_rs.at[m, n, 2 * l + h])
 
     for m, (w_in, w) in enumerate(((w1_in, w1), (w2_in, w2))):
-        weights_x(m, w_in, w, "wait")
-        for i in range(4):
-            weights_y(m, w, i).wait_send()
-            for s in range(2):
-                weights_core(m, w, s, i).wait_send()
+        for q in range(CUTS):
+            weights_x(m, q, w_in, w, "wait")
+            for i in range(4):
+                weights_y(m, q, w, i).wait_send()
+                for s in range(2):
+                    weights_core(m, q, w, s, i).wait_send()
     for k, (src, dst) in enumerate(((xs, x_all), (gs, g_all))):
-        swap_blocks(src, dst, every, a_ss.at[k], a_rs.at[k], "wait")
-        for g in range(4):
-            rows_y(k, dst, g).wait_send()
+        for q in range(CUTS):
+            swap_blocks(src, dst, cut(q), a_ss.at[k, q], a_rs.at[k, q], "wait")
+            for g in range(4):
+                rows_y(k, q, dst, g).wait_send()
     for k, (send, recv, fin, ret) in enumerate(((y_send, y_recv, y_fin, y_ret), (d_send, d_recv, d_fin, d_ret))):
         for h in range(len(SPANS)):
             swap_blocks(fin, ret, span(h), q_ss.at[k, h], q_rs.at[k, h], "wait")
@@ -434,20 +471,20 @@
         + [pltpu.VMEM((SLOTS, D), BF)] * 8
         + grad_scratch * 2
         + [
-            dma((2, NE)),
-            dma((2, NE)),
-            dma((2, 4)),
-            dma((2, 4)),
+            dma((2, CUTS, NE)),
+            dma((2, CUTS, NE)),
+            dma((2, CUTS, 4)),
+            dma((2, CUTS, 4)),
             dma((2, tiles)),
             dma((2, tiles)),
             dma((2, len(SPANS), NE)),
             dma((2, len(SPANS), NE)),
-            dma((2, 4)),
-            dma((2, 4)),
-            dma((2, 4)),
-            dma((2, 4)),
-            dma((2, 2, 4)),
-            dma((2, 2, 4)),
+            dma((2, CUTS, 4)),
+            dma((2, CUTS, 4)),
+            dma((2, CUTS, 4)),
+            dma((2, CUTS, 4)),
+            dma((2, CUTS, 2, 4)),
+            dma((2, CUTS, 2, 4)),
             dma((2, 2, tiles)),
             dma((2, 2, tiles)),
             dma((2, tiles)),

time: 118 us -> 111 us (0.941)
  Pallas kernels: 117 us -> 110 us
    pallas_call x1, Pallas kernels: 114 us -> 107 us  [body(): pl.pallas_call(kernel, out_shape=shapes, in_specs=[vmem] * 6 + [hbm] * 2,...]
where the time goes in v5:
time: 111 us; the launch traced here: 110 us
  Pallas kernels  110 us (99%)
    pallas_call x1, Pallas kernels, body(): pl.pallas_call(kernel, out_shape=shapes, in_specs=[vmem] * 6 + [hbm] * 2,...  107 us
    pallas_call x1, Pallas kernels, body(): pl.pallas_call(hand_out, out_shape=shapes, in_specs=[hbm] * 5, out_specs=...  3.02 us

profile of v5, /device:TPU:1, one launch (start us, length us, event | category | flops | bytes accessed | tf_op | source)
XLA Modules:
  0.0 110.3 jit_solution(13853721828445138158)
XLA Ops:
  0.6 106.7 %shard_map.119 = (bf16[128,1280]{1,0:T(8,128)(2,1)}, bf16[128,1280]{1,0:T(8,128)(2,1)}, f32[2,128]{1,0:T(2,128)}, bf16[2,160,1280]{2,1,0:T(8,128)(2,1)}, bf16[2,160,1280]{2,1,0:T(8,128)(2,1)}) custom-call(bf16[128,1280]{1,0:T(8,128)(2,1)} %tok.1, bf16[128,1280]{1,0:T(8,128)(2,1)} %cot.1, f32[2,128]{1,0:T(2,128)} %bitcast.3, s32[2,128]{1,0:T(2,128)} %bitcast.4, ...), custom_call_target="tpu_custom_call" | custom-call | tf_op jit(solution)/shard_map/pallas_call | solution.py:449
  107.3 3.0 %shard_map.120 = (bf16[128,1280]{1,0:T(8,128)(2,1)}, bf16[128,1280]{1,0:T(8,128)(2,1)}, f32[2,128]{1,0:T(2,128)}, bf16[2,160,1280]{2,1,0:T(8,128)(2,1)}, bf16[2,160,1280]{2,1,0:T(8,128)(2,1)}) custom-call(bf16[128,1280]{1,0:T(8,128)(2,1)} %get-tuple-element.15.refs_0_, bf16[128,1280]{1,0:T(8,128)(2,1)} %get-tuple-element.16.refs_1_, ...), custom_call_target="tpu_custom_call" | custom-call | tf_op jit(solution)/shard_map/pallas_call | solution.py:499

commit v6 on v5

--- a/solution.py
+++ b/solution.py
@@ -417,11 +417,16 @@
 
 def hand_out(*refs):
     sems = refs[-1]
-    half = len(refs) // 2
-    copies = [pltpu.make_async_copy(refs[i], refs[half + i], sems.at[i]) for i in range(half)]
-    for copy in copies:
+    ins, outs, held = refs[:5], refs[5:10], refs[10:15]
+    order = (2, 0, 1, 3, 4)
+    inward = [pltpu.make_async_copy(ins[i], held[i], sems.at[0, i]) for i in order]
+    outward = [pltpu.make_async_copy(held[i], outs[i], sems.at[1, i]) for i in order]
+    for copy in inward:
         copy.start()
-    for copy in copies:
+    for first, second in zip(inward, outward):
+        first.wait()
+        second.start()
+    for copy in outward:
         copy.wait()
 
 
@@ -500,8 +505,8 @@
         hand_out,
         out_shape=shapes,
         in_specs=[hbm] * 5,
-        out_specs=(vmem,) * 5,
-        scratch_shapes=[dma((5,))],
+        out_specs=(hbm,) * 5,
+        scratch_shapes=[pltpu.VMEM(one.shape, one.dtype) for one in shapes] + [dma((2, 5))],
     )(*results)
     return out, tg, gg.T, eg, rg
 

time: 111 us -> 110 us (level)
  no operation moved by 1% of the time
where the time goes in v6:
time: 110 us
  Pallas kernels  109 us (99%)
    pallas_call x1, Pallas kernels, body(): pl.pallas_call(kernel, out_shape=shapes, in_specs=[vmem] * 6 + [hbm] * 2,...  107 us
    pallas_call x1, Pallas kernels, body(): pl.pallas_call(hand_out, out_shape=shapes, in_specs=[hbm] * 5, out_specs=...  2.6 us

profile of v6, /device:TPU:1, one launch (start us, length us, event | category | flops | bytes accessed | tf_op | source)
XLA Modules:
  0.0 109.9 jit_solution(703000162940651665)
XLA Ops:
  0.6 106.7 %shard_map.119 = (bf16[128,1280]{1,0:T(8,128)(2,1)}, bf16[128,1280]{1,0:T(8,128)(2,1)}, f32[2,128]{1,0:T(2,128)}, bf16[2,160,1280]{2,1,0:T(8,128)(2,1)}, bf16[2,160,1280]{2,1,0:T(8,128)(2,1)}) custom-call(bf16[128,1280]{1,0:T(8,128)(2,1)} %tok.1, bf16[128,1280]{1,0:T(8,128)(2,1)} %cot.1, f32[2,128]{1,0:T(2,128)} %bitcast.3, s32[2,128]{1,0:T(2,128)} %bitcast.4, ...), custom_call_target="tpu_custom_call" | custom-call | tf_op jit(solution)/shard_map/pallas_call | solution.py:454
  107.3 2.6 %shard_map.120 = (bf16[128,1280]{1,0:T(8,128)(2,1)}, bf16[128,1280]{1,0:T(8,128)(2,1)}, f32[2,128]{1,0:T(2,128)}, bf16[2,160,1280]{2,1,0:T(8,128)(2,1)}, bf16[2,160,1280]{2,1,0:T(8,128)(2,1)}) custom-call(bf16[128,1280]{1,0:T(8,128)(2,1)} %get-tuple-element.15.refs_0_, bf16[128,1280]{1,0:T(8,128)(2,1)} %get-tuple-element.16.refs_1_, ...), custom_call_target="tpu_custom_call" | custom-call | tf_op jit(solution)/shard_map/pallas_call | solution.py:504
